TPU v7x, 256 devices: a whole 4x4x8 slice. The times are simulated.
256 devices in a mesh: row: 32 (over z, x), col: 8 (over y, core).
Axes of the slice: x: 4, y: 4, z: 8, core: 2. Of those that a mesh axis runs over, the one named last changes fastest.
Arguments:
- video: float32 [16384, 1024], P(('row', 'col')), may hold values from -0.6 to 0.6
- text: float32 [16384, 1024], P(('row', 'col')), may hold values from -0.6 to 0.6
- match_ids: int32 [16384], P(('row', 'col')), may hold values from 0 to 16383, as said below
- log_scale: float32 [1], replicated, may hold values from 2 to 2.7
- bias: float32 [1], replicated, may hold values from -8 to -4
Outputs:
- video_loss: float32 [16384], P(('row', 'col'))
- video_grad: float32 [16384, 1024], P(('row', 'col'))
- text_grad: float32 [16384, 1024], P(('row', 'col'))
Inputs may be any that keep to these rules, and one draw needn't show every extreme that they name: `match_ids`: a video row index.
All inputs are finite; a program needn't handle non-finite values.
Results may differ from a plain program's by a relative error of at most 0.0003.
Values sent between devices are 32-bit elements; how exact they have to be, the bound alone decides.
A program may use at most 64 MiB of HBM per device.

v0:
```python
import jax
import jax.numpy as jnp
from jax import lax
from jax.sharding import PartitionSpec as P

EPS = 1e-06
HIGH = lax.Precision.HIGHEST


def unit_rows(emb):
    inv = lax.rsqrt(jnp.sum(emb * emb, axis=1, keepdims=True) + EPS)
    return (emb * inv, inv)


def back_rows(unit, inv, grad):
    return (grad - unit * jnp.sum(unit * grad, axis=1, keepdims=True)) * inv


def pair_tile(video_all, video_index, text_all, ids_all, scale, shift):
    logits = lax.dot_general(
        video_all,
        text_all,
        (((1,), (1,)), ((), ())),
        precision=HIGH,
        preferred_element_type=jnp.float32,
    )
    logits = scale * logits + shift
    sign = jnp.where(ids_all[None, :] == video_index[:, None], 1.0, -1.0).astype(jnp.float32)
    margin = sign * logits
    loss = jnp.sum(jax.nn.softplus(-margin), axis=1)
    weight = -scale * sign * jax.nn.sigmoid(-margin)
    return (loss, weight)


def video_term(weight, text_all):
    return jnp.dot(weight, text_all, precision=HIGH, preferred_element_type=jnp.float32)


def text_term(weight, video_all):
    return lax.dot_general(
        weight,
        video_all,
        (((0,), (0,)), ((), ())),
        precision=HIGH,
        preferred_element_type=jnp.float32,
    )


def shards(video, text, match_ids, log_scale, bias):
    video_unit, video_inv = unit_rows(video)
    text_unit, text_inv = unit_rows(text)
    scale = jnp.exp(log_scale[0])
    shift = bias[0]
    rows = video.shape[0]
    col_count = lax.axis_size("col")
    row_place = lax.axis_index("row")
    video_all = lax.all_gather(video_unit, "col", axis=0, tiled=True)
    text_all, ids_all = (
        lax.all_gather(text_unit, "row", axis=0, tiled=True),
        lax.all_gather(match_ids, "row", axis=0, tiled=True),
    )
    local = jnp.arange(video_all.shape[0], dtype=jnp.int32)
    video_index = row_place * col_count * rows + local
    loss, weight = pair_tile(video_all, video_index, text_all, ids_all, scale, shift)
    video_loss = lax.psum_scatter(loss, "col", scatter_dimension=0, tiled=True)
    unit_vgrad = lax.psum_scatter(
        video_term(weight, text_all), "col", scatter_dimension=0, tiled=True
    )
    unit_tgrad = lax.psum_scatter(
        text_term(weight, video_all), "row", scatter_dimension=0, tiled=True
    )
    video_grad = back_rows(video_unit, video_inv, unit_vgrad)
    text_grad = back_rows(text_unit, text_inv, unit_tgrad)
    return (video_loss, video_grad, text_grad)


def solution(mesh):
    return jax.shard_map(
        shards,
        mesh=mesh,
        in_specs=(P(("row", "col"), None), P(("row", "col"), None), P(("row", "col")), P(), P()),
        out_specs=(P(("row", "col")), P(("row", "col"), None), P(("row", "col"), None)),
        check_vma=False,
    )
```

profile of v0, /device:TPU:1, one launch (start us, length us, event | category | flops | bytes accessed | tf_op | source)
XLA Modules:
  0.0 451.6 jit_solution(7988637225066689654)
XLA Ops:
  7.2 1.1 multiply_reduce_fusion.3
  8.3 1.7 broadcast_multiply_fusion.1
  10.1 1.1 multiply_reduce_fusion.2
  11.2 1.7 broadcast_multiply_fusion
  13.0 0.0 reduce-scatter.3.cloned.1.call-start
  14.4 1.3 dynamic-slice
  16.3 0.9 dynamic-update-slice
  17.2 20.5 %all-reduce = s32[2048]{0:T(1024)S(1)} all-reduce(s32[2048]{0:T(1024)S(1)} %dynamic-update-slice), channel_id=1, replica_groups=mesh['row'=32,'col'=8] {'row'}, use_global_device_ids=true, to_apply=%add | all-reduce | flops 2048 | bytes 16384
  37.7 4.8 %all-gather.3.cloned.1.call-done = f32[512,1024]{1,0:T(8,128)} async-done(((f32[64,1024]{1,0:T(8,128)}), f32[512,1024]{1,0:T(8,128)}) %all-gather.3.cloned.1.call-update) | async-done | bytes 2097168 | tf_op jit(solution)/shard_map/all_gather | solution.py:57
  42.4 101.0 %all-gather.5.cloned.1.call-done = f32[2048,1024]{1,0:T(8,128)} async-done(((f32[64,1024]{1,0:T(8,128)}), f32[2048,1024]{1,0:T(8,128)}) %all-gather.5.cloned.1.call-update) | async-done | bytes 8388624 | tf_op jit(solution)/shard_map/all_gather | solution.py:59
  143.4 19.3 %fusion.1 = (f32[512]{0:T(512)S(1)}, f32[512,2048]{1,0:T(8,128)S(1)}) fusion(f32[]{:T(128)} %bitcast.8, f32[512,1024]{1,0:T(8,128)} %all-gather.3.cloned.1.call-done, f32[2048,1024]{1,0:T(8,128)} %all-gather.5.cloned.1.call-done, f32[]{:T(128)} %bitcast.1, s32[512]{0:T(512)S(1)} %iota_add_fusion, s32[2048]{0:T(1024)S(1)} %all-reduce), kind=kOutput, calls=%fused_computation.4 | convolution fusion | flops 12898533376 | bytes 14692360 | tf_op jit(solution)/shard_map/dot_general | solution.py:20
  162.8 2.0 copy-done.5
  164.7 15.9 %fusion.4 = f32[512,1024]{1,0:T(8,128)} fusion(f32[2048,1024]{1,0:T(8,128)S(1)} %copy-done.2, f32[512,2048]{1,0:T(8,128)S(1)} %get-tuple-element.4, f32[]{:T(128)S(6)} %neg.14, s32[2048]{0:T(1024)S(1)} %all-reduce, s32[512]{0:T(512)S(1)} %iota_add_fusion), kind=kOutput, calls=%fused_computation.17 | convolution fusion | flops 12891193344 | bytes 14690308 | tf_op jit(solution)/shard_map/dot_general | solution.py:36
  180.6 0.0 reduce-scatter.5.cloned.1.call-start
  180.7 17.9 %fusion.2 = f32[2048,1024]{1,0:T(8,128)} fusion(f32[512,1024]{1,0:T(8,128)S(1)} %copy-done.3, f32[512,2048]{1,0:T(8,128)} %copy-done.5, f32[]{:T(128)S(6)} %neg.14, s32[2048]{0:T(1024)S(1)} %all-reduce, s32[512]{0:T(512)S(1)} %iota_add_fusion), kind=kOutput, calls=%fused_computation.16 | convolution fusion | flops 12891193344 | bytes 14690308 | tf_op jit(solution)/shard_map/dot_general | solution.py:40
  198.7 0.6 copy-done.4
  199.3 0.6 dynamic-slice.1
  200.5 12.9 %all-reduce.1 = f32[512]{0:T(512)S(1)} all-reduce(f32[512]{0:T(512)S(1)} %get-tuple-element.3), channel_id=2, replica_groups=mesh['row'=32,'col'=8] {'col'}, use_global_device_ids=true, to_apply=%region_3.4.clone | all-reduce | flops 512 | bytes 4096
  213.4 0.6 dynamic-slice.2
  214.0 1.2 multiply_reduce_fusion.1
  215.2 1.8 subtract_multiply_fusion.1
  217.0 225.1 %reduce-scatter.5.cloned.1.call-done = f32[64,1024]{1,0:T(8,128)} async-done(((f32[2048,1024]{1,0:T(8,128)}), f32[64,1024]{1,0:T(8,128)}) %reduce-scatter.5.cloned.1.call-update) | async-done | bytes 262160 | tf_op jit(solution)/shard_map/reduce_scatter | solution.py:69
  442.1 1.2 multiply_reduce_fusion
  443.3 1.8 subtract_multiply_fusion
  (21 shorter events, 0.2 us)
Async XLA Ops:
  7.2 35.3 %all-gather.3.cloned.1.call-start = ((), (), s32[]{:S(2)}) async-start(), calls=%async_computation.2 | async-start | bytes 2359296 | tf_op jit(solution)/shard_map/all_gather | solution.py:57
  10.1 133.3 %all-gather.5.cloned.1.call-start = ((), (), s32[]{:S(2)}) async-start(), calls=%async_computation.3 | async-start | bytes 8650752 | tf_op jit(solution)/shard_map/all_gather | solution.py:59
  13.0 201.0 %reduce-scatter.3.cloned.1.call-start = ((), (), s32[]{:S(2)}) async-start(), calls=%async_computation.4 | async-start | bytes 2359296 | tf_op jit(solution)/shard_map/reduce_scatter | solution.py:66
  143.4 21.3 %copy-start.2 = (f32[2048,1024]{1,0:T(8,128)S(1)}, f32[2048,1024]{1,0:T(8,128)}, u32[]{:S(2)}) copy-start(f32[2048,1024]{1,0:T(8,128)} %all-gather.5.cloned.1.call-done) | copy-start | bytes 25165828
  162.7 2.0 copy-start.5
  164.7 15.9 %copy-start.3 = (f32[512,1024]{1,0:T(8,128)S(1)}, f32[512,1024]{1,0:T(8,128)}, u32[]{:S(2)}) copy-start(f32[512,1024]{1,0:T(8,128)} %all-gather.3.cloned.1.call-done) | copy-start | bytes 6291460
  180.6 261.5 %reduce-scatter.5.cloned.1.call-start = ((), (), s32[]{:S(2)}) async-start(), calls=%async_computation.5 | async-start | bytes 8650752 | tf_op jit(solution)/shard_map/reduce_scatter | solution.py:69
  198.6 0.7 copy-start.4
  198.6 15.4 %copy-start = (f32[64,1024]{1,0:T(8,128)S(1)}, f32[64,1024]{1,0:T(8,128)}, u32[]{:S(2)}) copy-start(f32[64,1024]{1,0:T(8,128)} %param.5) | copy-start | bytes 786436
  198.6 243.5 %copy-start.1 = (f32[64,1024]{1,0:T(8,128)S(1)}, f32[64,1024]{1,0:T(8,128)}, u32[]{:S(2)}) copy-start(f32[64,1024]{1,0:T(8,128)} %param.6) | copy-start | bytes 786436
Sparse Core Ops, SparseCore 0:
  10.4 31.9 all-gather.2
  45.6 97.7 all-gather.4
  180.7 31.0 reduce-scatter.2
  215.7 226.3 reduce-scatter.4
where the time goes:
time: 455 us; the launch traced here: 452 us
  waiting for transfers between devices  331 us (73%)
  matrix products  53.1 us (12%)
  blocking collectives  33.4 us (7%)
  between operations  16.5 us (4%)
  other arithmetic  11.5 us (3%)
  local copies, waits for them, and re-layouts  5.95 us (1%)
    reduce_scatter x1, waiting for transfers between devices, shards(): lax.psum_scatter(text_term(weight, video_all), 'row', scatter_dimension=0...  225 us
    all_gather x1, waiting for transfers between devices, shards(): lax.all_gather(text_unit, 'row', axis=0, tiled=True)  101 us
    unnamed x2, blocking collectives  33.4 us
    dot_general x1, matrix products, pair_tile(): lax.dot_general(video_all, text_all, (((1,), (1,)), ((), ())), precision=...  19.3 us
    dot_general x1, matrix products, text_term(): lax.dot_general(weight, video_all, (((0,), (0,)), ((), ())), precision=HI...  17.9 us
    dot_general x1, matrix products, video_term(): jnp.dot(weight, text_all, precision=HIGH, preferred_element_type=jnp.floa...  15.9 us
  transfers between devices with their start and end apart: 4, of which 3 were waited for; matrix products, arithmetic and copies ran while one was open for 6% of the time, Pallas kernels for 0%

commit v1 on v0

v1 whole, which is shorter than its diff:
```python
import jax
import jax.numpy as jnp
from jax import lax
from jax.experimental import pallas as pl
from jax.experimental.pallas import tpu as pltpu
from jax.sharding import PartitionSpec as P

EPS = 1e-06
MESH = pl.DeviceIdType.MESH
F32 = jnp.float32
BF16 = jnp.bfloat16


def dot_nn(a, b):
    return lax.dot_general(a, b, (((1,), (0,)), ((), ())), preferred_element_type=F32)


def dot_nt(a, b):
    return lax.dot_general(a, b, (((1,), (1,)), ((), ())), preferred_element_type=F32)


def dot_tn(a, b):
    return lax.dot_general(a, b, (((0,), (0,)), ((), ())), preferred_element_type=F32)


def split(x):
    hi = x.astype(BF16)
    return hi, (x - hi.astype(F32)).astype(BF16)


def rows(start, size):
    if not isinstance(start, int):
        start = pl.multiple_of(start, size)
    return pl.ds(start, size)


def kernel(
    video_ref, text_ref, ids_ref, log_scale_ref, bias_ref,
    loss_ref, vgrad_ref, tgrad_ref,
    vf, tf, vh, vl, th, tl, w, vg, tg, recv_t, recv_v, recv_s, ids_slot, ids_vec, vidx, lacc, lrow, lrecv, inv_v, inv_t,
    t_send, t_recv, z_send, z_recv, s_send, s_recv, i_send, i_recv,
    rt_send, rt_recv, rz_send, rz_recv, rs_send, rs_recv, l_send, l_recv,
):
    row, col = lax.axis_index("row"), lax.axis_index("col")
    z, x, y, core = row // 4, row % 4, col // 2, col % 2
    diag = (x + y) % 4

    def at(x_, y_, z_, core_):
        return (z_ * 4 + x_, y_ * 2 + core_)

    xp, xm, yp, ym = (x + 1) % 4, (x + 3) % 4, (y + 1) % 4, (y + 3) % 4
    next_a = at(jnp.where(diag == 3, x, xp), jnp.where(diag == 3, yp, y), z, core)
    next_b = at(jnp.where(diag == 3, xp, x), jnp.where(diag == 3, y, yp), z, core)
    prev_a = at(jnp.where(diag == 0, x, xm), jnp.where(diag == 0, ym, y), z, core)
    prev_b = at(jnp.where(diag == 0, xm, x), jnp.where(diag == 0, y, ym), z, core)
    t_out = (next_a, prev_a, next_b, prev_b)
    t_back = (prev_a, next_a, prev_b, next_b)
    z_out = (at(x, y, (z + 1) % 8, core), at(x, y, (z + 7) % 8, core))
    z_back = (z_out[1], z_out[0])
    other = at(x, y, z, 1 - core)

    barrier = pltpu.get_barrier_semaphore()
    for peer in t_out:
        pl.semaphore_signal(barrier, inc=1, device_id=peer, device_id_type=MESH)
    pl.semaphore_signal(barrier, inc=1, device_id=other, device_id_type=MESH)
    for step in range(1, 8):
        for c in range(2):
            pl.semaphore_signal(barrier, inc=1, device_id=at(x, y, (z + step) % 8, c), device_id_type=MESH)

    def unit(ref, inv_ref):
        full = ref[...]
        inv = lax.rsqrt(jnp.sum(full * full, axis=1, keepdims=True) + EPS)
        inv_ref[...] = jnp.broadcast_to(inv, (64, 128))
        return full * inv

    tu = unit(text_ref, inv_t)
    tf[rows(896, 64), :] = tu
    hi, lo = split(tu)
    th[rows(896, 64), :] = hi
    tl[rows(896, 64), :] = lo
    vu = unit(video_ref, inv_v)
    hi, lo = split(vu)
    for half in range(2):
        vf[rows(768 + 128 * half, 32), :] = vu[32 * half : 32 * half + 32]
        vh[rows(768 + 128 * half, 32), :] = hi[32 * half : 32 * half + 32]
        vl[rows(768 + 128 * half, 32), :] = lo[32 * half : 32 * half + 32]

    def t_copy(way, tick, src, dst):
        return pltpu.make_async_remote_copy(
            src_ref=tf.at[rows(src, 16)], dst_ref=tf.at[rows(dst, 16)],
            send_sem=t_send.at[way], recv_sem=t_recv.at[way, tick],
            device_id=t_out[way], device_id_type=MESH,
        )

    def z_copy(way, tick, src, dst):
        return pltpu.make_async_remote_copy(
            src_ref=vf.at[rows(src, 16)], dst_ref=vf.at[rows(dst, 16)],
            send_sem=z_send.at[way], recv_sem=z_recv.at[way, tick],
            device_id=z_out[way], device_id_type=MESH,
        )

    def s_copy(way, tick, src):
        return pltpu.make_async_remote_copy(
            src_ref=vf.at[rows(src, 16)], dst_ref=vf.at[rows(src + 32, 16)],
            send_sem=s_send.at[way], recv_sem=s_recv.at[way, tick],
            device_id=other, device_id_type=MESH,
        )

    def i_copy(way, step, src):
        return pltpu.make_async_remote_copy(
            src_ref=src, dst_ref=ids_slot.at[way, step],
            send_sem=i_send.at[way], recv_sem=i_recv.at[way, step],
            device_id=t_out[way], device_id_type=MESH,
        )

    pl.semaphore_wait(barrier, 19)

    for way in range(4):
        i_copy(way, 0, ids_ref.at[way // 2]).start()
    for part in range(2):
        for way in range(4):
            t_copy(way, part, 896 + 32 * (way // 2) + 16 * part, 32 * way + 16 * part).start()
        for way in range(2):
            for q in (2 * part, 2 * part + 1):
                z_copy(way, q, 768 + 128 * (q // 2) + 16 * (q % 2), 128 * (q // 2) + 64 * way + 16 * (q % 2)).start()
    for q in range(4):
        s_copy(q // 2, 14 + q % 2, 768 + 128 * (q // 2) + 16 * (q % 2)).start()

    local = lax.broadcasted_iota(jnp.int32, (32, 128), 0)
    for hg in range(4):
        for half in range(2):
            for way in range(2):
                for who in range(2):
                    if hg < 3:
                        from_z = (z + (7 - hg if way == 0 else hg + 1)) % 8
                    else:
                        from_z = (z + 4 * way) % 8
                    from_core = core if who == 0 else 1 - core
                    base = ((from_z * 4 + x) * 8 + y * 2 + from_core) * 64 + 32 * half
                    vidx[rows(256 * hg + 128 * half + 64 * way + 32 * who, 32), :] = local + base
    lacc[...] = jnp.zeros_like(lacc)

    scale = jnp.exp(jnp.full((1, 128), log_scale_ref[0], F32))
    bias = jnp.full((1, 128), bias_ref[0], F32)
    lane = lax.broadcasted_iota(jnp.int32, (1, 128), 1)

    def t_split(start, size):
        hi, lo = split(tf[rows(start, size), :])
        th[rows(start, size), :] = hi
        tl[rows(start, size), :] = lo

    def v_split(start, size):
        hi, lo = split(vf[rows(start, size), :])
        vh[rows(start, size), :] = hi
        vl[rows(start, size), :] = lo

    def v_slot(tick, way):
        q = tick % 4
        return 256 * (tick // 4) + 128 * (q // 2) + 64 * way + 16 * (q % 2)

    def block(n):
        m = (n >= 1).astype(jnp.int32) + (n >= 4).astype(jnp.int32) + (n >= 9).astype(jnp.int32)
        r = n - m * m
        vb = jnp.where(r <= m, r, m)
        tb = jnp.where(r <= m, m, r - m - 1)
        vs, ts = rows(vb * 256, 256), rows(tb * 256, 256)
        dots = dot_nt(vh[vs, :], th[ts, :]) + (dot_nt(vh[vs, :], tl[ts, :]) + dot_nt(vl[vs, :], th[ts, :]))
        total = jnp.zeros((256, 128), F32)
        for half in range(2):
            logits = dots[:, 128 * half : 128 * half + 128] * scale + bias
            match = vidx[vs, :] == ids_vec[tb * 2 + half]
            q = jnp.where(match, -logits, logits)
            e = jnp.exp(q)
            u = 1.0 + e
            weight = (jnp.where(match, -scale, scale) * e) / u
            small = e * (1.0 - e * (0.5 - e * (1.0 / 3.0)))
            total = total + jnp.where(e < 1.0 / 64.0, small, jnp.log(u))
            hi, lo = split(weight)
            cols = pl.ds(pl.multiple_of((tb * 2 + half) * 128, 128), 128)
            for k in range(2):
                w[vb * 2 + k, 0, :, cols] = hi[128 * k : 128 * k + 128]
                w[vb * 2 + k, 1, :, cols] = lo[128 * k : 128 * k + 128]
        lacc[vs, :] += total

    def count(tick):
        done = 0
        for bound, more in ((4, 1), (8, 1), (9, 1), (10, 1), (12, 2), (13, 2), (14, 8)):
            done = done + jnp.where(tick >= bound, more, 0)
        return done

    @pl.loop(0, 15)
    def _(tick):
        part = tick % 2
        step = tick // 2
        base = 128 * step + 16 * part

        @pl.when(tick < 14)
        def _():
            for way in range(4):
                slot = base + 32 * way
                t_copy(way, tick, slot, slot).wait_recv()

                @pl.when(tick < 12)
                def _():
                    t_copy(way, tick + 2, slot, slot + 128).start()

                @pl.when((tick >= 12) & (part == way % 2))
                def _():
                    t_copy(way, 14, slot, 960 + 32 * (way // 2) + 16 * (way % 2)).start()

            @pl.when(part == 0)
            def _():
                for way in range(4):
                    i_copy(way, step, ids_slot.at[way, step]).wait_recv()

                    @pl.when(tick < 12)
                    def _():
                        i_copy(way, step + 1, ids_slot.at[way, step]).start()

                    if way % 2 == 0:

                        @pl.when(tick == 12)
                        def _():
                            i_copy(way, 7, ids_slot.at[way, step]).start()

                ids_vec[step] = jnp.where(
                    lane < 64,
                    jnp.where(lane < 32, ids_slot[0, step], ids_slot[1, step]),
                    jnp.where(lane < 96, ids_slot[2, step], ids_slot[3, step]),
                )

        @pl.when(tick == 14)
        def _():
            for way in range(4):
                slot = 960 + 32 * (way // 2) + 16 * (way % 2)
                t_copy(way, 14, slot, slot).wait_recv()
            for way in (0, 2):
                i_copy(way, 7, ids_slot.at[way, 7]).wait_recv()
            ids_vec[7] = jnp.where(
                lane < 64,
                jnp.where(lane < 32, ids_ref[0], ids_ref[1]),
                jnp.where(lane < 96, ids_slot[0, 7], ids_slot[2, 7]),
            )

        for way in range(2):

            @pl.when(tick < 12)
            def _():
                slot = v_slot(tick, way)
                z_copy(way, tick, slot, slot).wait_recv()

                @pl.when(tick < 8)
                def _():
                    z_copy(way, tick + 4, slot, slot + 256).start()

                @pl.when((tick >= 8) & ((tick % 4) // 2 == way))
                def _():
                    last = 768 + 128 * way + 64 + 16 * (tick % 2)
                    z_copy(way, 12 + tick % 2, slot, last).start()

                s_copy(way, tick, slot).start()

            @pl.when((tick == 12) | (tick == 13))
            def _():
                slot = 768 + 128 * way + 64 + 16 * (tick % 2)
                z_copy(way, tick, slot, slot).wait_recv()
                s_copy(way, tick, slot).start()

            @pl.when((tick >= 1) & (tick <= 12))
            def _():
                slot = v_slot(tick - 1, way)
                s_copy(way, tick - 1, slot).wait_recv()
                v_split(slot + 32, 16)

            @pl.when(tick >= 13)
            def _():
                slot = 768 + 128 * way + 64 + 16 * ((tick - 1) % 2)
                s_copy(way, tick - 1, slot).wait_recv()
                v_split(slot + 32, 16)

            @pl.when(tick < 12)
            def _():
                v_split(v_slot(tick, way), 16)

            @pl.when((tick == 12) | (tick == 13))
            def _():
                v_split(768 + 128 * way + 64 + 16 * (tick % 2), 16)

            @pl.when(tick == 0)
            def _():
                for part_ in range(2):
                    slot = 768 + 128 * way + 16 * part_
                    s_copy(way, 14 + part_, slot).wait_recv()
                    v_split(slot + 32, 16)

        @pl.when(tick < 14)
        def _():
            for way in range(4):
                t_split(base + 32 * way, 16)

        @pl.when(tick == 14)
        def _():
            t_split(960, 64)

        @pl.loop(count(tick - 1), count(tick))
        def _(n):
            block(n)

    def rt_copy(way, part, step, src, dst):
        return pltpu.make_async_remote_copy(
            src_ref=tg.at[rows(src, 16)], dst_ref=recv_t.at[rows(dst, 16)],
            send_sem=rt_send.at[way], recv_sem=rt_recv.at[way, part, step],
            device_id=t_back[way], device_id_type=MESH,
        )

    def rt_slot(way, part, step):
        return jnp.where(step == 0, 896, 128 * (step - 1)) + 32 * way + 16 * part

    def t_pump(step, part, first):
        for way in range(4):
            slot = 128 * (step - 1) + 32 * way + 16 * part
            if not first or way % 2 == part:
                rt_copy(way, part, step, slot, slot).wait_recv()
                tg[rows(slot, 16), :] += recv_t[rows(slot, 16), :]
            rt_copy(way, part, step - 1, slot, rt_slot(way, part, step - 1)).start()

    def rz_copy(way, half, step, src):
        return pltpu.make_async_remote_copy(
            src_ref=vg.at[rows(src, 32)], dst_ref=recv_v.at[step, half, way],
            send_sem=rz_send.at[way], recv_sem=rz_recv.at[way, half, step],
            device_id=z_back[way], device_id_type=MESH,
        )

    def rs_copy(hg, half, way):
        src = 256 * hg + 128 * half + 64 * way + 32
        return pltpu.make_async_remote_copy(
            src_ref=vg.at[rows(src, 32)], dst_ref=recv_s.at[hg, half, way],
            send_sem=rs_send.at[0], recv_sem=rs_recv.at[hg, half, way],
            device_id=other, device_id_type=MESH,
        )

    def z_pump(hg, half, with_recv):
        for way in range(2):
            slot = 256 * hg + 128 * half + 64 * way
            rs_copy(hg, half, way).wait_recv()
            if with_recv[way]:
                rz_copy(way, half, hg + 1, slot).wait_recv()
                vg[rows(slot, 32), :] += recv_s[hg, half, way] + recv_v[hg + 1, half, way]
            else:
                vg[rows(slot, 32), :] += recv_s[hg, half, way]
            rz_copy(way, half, hg, slot).start()

    def z_last(half):
        slot = 768 + 128 * half + 64
        rs_copy(3, half, 1).wait_recv()
        vg[rows(slot, 32), :] += recv_s[3, half, 1]
        rz_copy(half, half, 3, slot).start()

    def t_grad(g):
        cols = pl.ds(pl.multiple_of(g * 128, 128), 128)
        hi = w[:, 0, :, cols].reshape(1024, 128)
        lo = w[:, 1, :, cols].reshape(1024, 128)
        both = dot_tn(jnp.concatenate([hi, lo], axis=1), vh[...])
        tg[rows(g * 128, 128), :] = both[:128] + (both[128:] + dot_tn(hi, vl[...]))

    def v_grad(m):
        both = dot_nn(w[m].reshape(256, 1024), th[...])
        vg[rows(m * 128, 128), :] = both[:128] + (both[128:] + dot_nn(w[m, 0], tl[...]))

    def l_copy(hg, way, who, owner):
        slot = (hg * 2 + way) * 2 + who
        return pltpu.make_async_remote_copy(
            src_ref=lrow.at[hg], dst_ref=lrecv.at[slot],
            send_sem=l_send.at[0], recv_sem=l_recv.at[slot],
            device_id=owner, device_id_type=MESH,
        )

    def l_peers():
        peers = []
        for hg in range(4):
            for way in range(2):
                if hg < 3:
                    to_z = (z + (7 - hg if way == 0 else hg + 1)) % 8
                else:
                    to_z = (z + 4 * way) % 8
                for who in range(2):
                    if (hg, way, who) != (3, 0, 0):
                        peers.append((hg, way, who, at(x, y, to_z, core if who == 0 else 1 - core)))
        return peers

    @pl.loop(0, 8)
    def _(i):
        t_grad(7 - i)

        @pl.when(i == 0)
        def _():
            for way in range(4):
                part = way % 2
                src = 960 + 32 * (way // 2) + 16 * part
                rt_copy(way, part, 7, src, 768 + 32 * way + 16 * part).start()

        @pl.when(i == 1)
        def _():
            t_pump(7, 0, True)
            z_last(0)

        @pl.when(i >= 2)
        def _():
            t_pump(8 - i, 0, False)

        @pl.when(i == 2)
        def _():
            z_last(1)

        @pl.when(i == 3)
        def _():
            z_pump(2, 0, (True, False))

        @pl.when(i == 4)
        def _():
            z_pump(2, 1, (False, True))

        @pl.when(i >= 5)
        def _():
            z_pump(2 - (i - 3) // 2, (i - 3) % 2, (True, True))

        hg, half = 3 - i // 2, i % 2
        v_grad(2 * hg + half)
        for way in range(2):
            rs_copy(hg, half, way).start()

        @pl.when(i == 1)
        def _():
            t_pump(7, 1, True)

        @pl.when(i >= 2)
        def _():
            t_pump(8 - i, 1, False)

        @pl.when(i == 3)
        def _():
            for m in range(8):
                turned = jnp.transpose(lacc[rows(m * 128, 128), :])
                lrow[m // 2, m % 2 : m % 2 + 1, :] = jnp.sum(turned, axis=0, keepdims=True)
            for hg_, way, who, owner in l_peers():
                l_copy(hg_, way, who, owner).start()

    z_pump(0, 1, (True, True))

    loss = lrow[3][:, :32]
    for hg, way, who, owner in l_peers():
        l_copy(hg, way, who, owner).wait_recv()
        first = 64 * way + 32 * who
        loss = loss + lrecv[(hg * 2 + way) * 2 + who][:, first : first + 32]
    loss_ref[...] = loss

    for ring in range(2):
        for part in range(2):
            own = 896 + 32 * ring + 16 * part
            total = tg[rows(own, 16), :]
            for way in (2 * ring, 2 * ring + 1):
                slot = 896 + 32 * way + 16 * part
                rt_copy(way, part, 0, own, slot).wait_recv()
                total = total + recv_t[rows(slot, 16), :]
            u = tf[rows(own, 16), :]
            first = 32 * ring + 16 * part
            back = total - u * jnp.sum(u * total, axis=1, keepdims=True)
            tgrad_ref[rows(first, 16), :] = back * inv_t[rows(first, 16), :1]

    for half in range(2):
        own = 768 + 128 * half
        rs_copy(3, half, 0).wait_recv()
        total = vg[rows(own, 32), :] + recv_s[3, half, 0]
        for way in range(2):
            rz_copy(way, half, 0, own).wait_recv()
            total = total + recv_v[0, half, way]
        u = vf[rows(own, 32), :]
        back = total - u * jnp.sum(u * total, axis=1, keepdims=True)
        vgrad_ref[rows(32 * half, 32), :] = back * inv_v[rows(32 * half, 32), :1]

    def drain(ref, sem):
        pltpu.make_async_remote_copy(
            src_ref=ref, dst_ref=ref, send_sem=sem, recv_sem=sem, device_id=other, device_id_type=MESH
        ).wait_send()

    for way in range(4):
        drain(tf.at[rows(0, 240)], t_send.at[way])
        drain(tg.at[rows(0, 240)], rt_send.at[way])
        drain(ids_slot.at[way, pl.ds(0, 8 if way % 2 == 0 else 7)], i_send.at[way])
    for way in range(2):
        drain(vf.at[rows(0, 224)], z_send.at[way])
        drain(vf.at[rows(0, 256)], s_send.at[way])
        drain(vg.at[rows(0, 224)], rz_send.at[way])
    drain(vg.at[rows(0, 512)], rs_send.at[0])
    drain(lrecv.at[pl.ds(0, 15)], l_send.at[0])


def shards(video, text, match_ids, log_scale, bias):
    ids = jnp.tile(match_ids.reshape(2, 1, 32), (1, 1, 4))
    vmem = pl.BlockSpec(memory_space=pltpu.VMEM)
    smem = pl.BlockSpec(memory_space=pltpu.SMEM)
    dma = pltpu.SemaphoreType.DMA
    loss, vgrad, tgrad = pl.pallas_call(
        kernel,
        out_shape=(
            jax.ShapeDtypeStruct((2, 32), F32),
            jax.ShapeDtypeStruct((64, 1024), F32),
            jax.ShapeDtypeStruct((64, 1024), F32),
        ),
        in_specs=[vmem, vmem, vmem, smem, smem],
        out_specs=(vmem, vmem, vmem),
        scratch_shapes=[
            pltpu.VMEM((1024, 1024), F32),
            pltpu.VMEM((1024, 1024), F32),
            pltpu.VMEM((1024, 1024), BF16),
            pltpu.VMEM((1024, 1024), BF16),
            pltpu.VMEM((1024, 1024), BF16),
            pltpu.VMEM((1024, 1024), BF16),
            pltpu.VMEM((8, 2, 128, 1024), BF16),
            pltpu.VMEM((1024, 1024), F32),
            pltpu.VMEM((1024, 1024), F32),
            pltpu.VMEM((1024, 1024), F32),
            pltpu.VMEM((4, 2, 2, 32, 1024), F32),
            pltpu.VMEM((4, 2, 2, 32, 1024), F32),
            pltpu.VMEM((4, 8, 1, 128), jnp.int32),
            pltpu.VMEM((8, 1, 128), jnp.int32),
            pltpu.VMEM((1024, 128), jnp.int32),
            pltpu.VMEM((1024, 128), F32),
            pltpu.VMEM((4, 2, 128), F32),
            pltpu.VMEM((16, 2, 128), F32),
            pltpu.VMEM((64, 128), F32),
            pltpu.VMEM((64, 128), F32),
            dma((4,)), dma((4, 15)),
            dma((2,)), dma((2, 14)),
            dma((2,)), dma((2, 16)),
            dma((4,)), dma((4, 8)),
            dma((4,)), dma((4, 2, 8)),
            dma((2,)), dma((2, 2, 4)),
            dma((1,)), dma((4, 2, 2)),
            dma((1,)), dma((16,)),
        ],
        compiler_params=pltpu.CompilerParams(
            collective_id=0, has_side_effects=True, vmem_limit_bytes=56 * 2**20
        ),
        cost_estimate=pl.CostEstimate(flops=18 * 2**30, bytes_accessed=2**20, transcendentals=3 * 2**20),
    )(video, text, ids, log_scale, bias)
    return loss.reshape(64), vgrad, tgrad


def solution(mesh):
    return jax.shard_map(
        shards,
        mesh=mesh,
        in_specs=(P(("row", "col"), None), P(("row", "col"), None), P(("row", "col")), P(), P()),
        out_specs=(P(("row", "col")), P(("row", "col"), None), P(("row", "col"), None)),
        check_vma=False,
    )
```

time: 455 us -> 100 us (0.22)
  waiting for transfers between devices: 331 us -> 0 us
  Pallas kernels: 0 us -> 93.6 us
  matrix products: 53.1 us -> 0 us
  blocking collectives: 33.4 us -> 0 us
  between operations: 16.5 us -> 1.97 us
  other arithmetic: 11.5 us -> 0 us
    reduce_scatter x2 -> x0, waiting for transfers between devices: 225 us -> none  [the longest x1 225 us: shards(): lax.psum_scatter(text_term(weight, video_all), 'row', scatter_dimension=0...]
    all_gather x2 -> x0, waiting for transfers between devices: 106 us -> none  [the longest x1 101 us: shards(): lax.all_gather(text_unit, 'row', axis=0, tiled=True)]
    pallas_call x0 -> x1, Pallas kernels: none -> 93.6 us  [shards(): pl.pallas_call(kernel, out_shape=(jax.ShapeDtypeStruct((2, 32), F32), jax...]
    dot_general x3 -> x0, matrix products: 53.1 us -> none  [the longest x1 19.3 us: pair_tile(): lax.dot_general(video_all, text_all, (((1,), (1,)), ((), ())), precision=...]
    unnamed x2 -> x0, blocking collectives: 33.4 us -> none
    mul x4 -> x0, other arithmetic: 7.04 us -> none  [the longest x2 3.54 us: back_rows(): return (grad - unit * jnp.sum(unit * grad, axis=1, keepdims=True)) * inv]
  transfers between devices with their start and end apart: 4 -> 0, of which waited for: 3 -> 0; matrix products, arithmetic and copies ran while one was open for 6% -> 0% of each run, Pallas kernels for 0% -> 0%
where the time goes in v1:
time: 100 us; the launch traced here: 99.9 us
  Pallas kernels  93.6 us (94%)
  local copies, waits for them, and re-layouts  4.41 us (4%)
  between operations  1.97 us (2%)
    pallas_call x1, Pallas kernels, shards(): pl.pallas_call(kernel, out_shape=(jax.ShapeDtypeStruct((2, 32), F32), jax...  93.6 us
    unnamed x8, local copies, waits for them, and re-layouts  3.08 us

profile of v1, /device:TPU:1, one launch (start us, length us, event | category | flops | bytes accessed | tf_op | source)
XLA Modules:
  0.0 99.9 jit_solution(9774447959573404425)
XLA Ops:
  1.3 0.0 copy-start.1
  1.9 0.0 copy-done.1
  2.0 0.1 tile.10
  2.0 0.6 tile.12.ids_ref
  2.7 93.6 %shard_map.76 = (f32[2,32]{1,0:T(2,128)}, f32[64,1024]{1,0:T(8,128)}, f32[64,1024]{1,0:T(8,128)}) custom-call(f32[64,1024]{1,0:T(8,128)} %video_ref.1, f32[64,1024]{1,0:T(8,128)} %text_ref.1, s32[2,1,128]{2,1,0:T(1,128)} %tile.12.ids_ref, f32[1]{0:T(128)S(6)} %copy.10.log_scale_ref, f32[1]{0:T(128)S(6)} %copy.11.bias_ref), custom_call_target="tpu_custom_call" | custom-call | flops 19327352832 | bytes 1048576 | tf_op jit(solution)/shard_map/pallas_call | solution.py:503
  96.3 0.0 copy-start.2
  96.3 0.7 copy-done.2
  96.9 0.6 reshape.15
  97.5 0.0 copy-start
  97.5 1.7 %copy.12 = f32[64,1024]{1,0:T(8,128)} copy(f32[64,1024]{1,0:T(8,128)} %get-tuple-element.13) | data formatting | bytes 524288
  99.2 0.0 copy-done
  99.2 0.7 copy.13
  (1 shorter events, 0.0 us)
Async XLA Ops:
  1.3 0.7 copy-start.1
  96.3 0.7 copy-start.2
  97.5 1.7 %copy-start = (f32[64,1024]{1,0:T(8,128)S(1)}, f32[64,1024]{1,0:T(8,128)}, u32[]{:S(2)}) copy-start(f32[64,1024]{1,0:T(8,128)} %get-tuple-element.14) | copy-start | bytes 786436

commit v2 on v1

--- a/solution.py
+++ b/solution.py
@@ -11,6 +11,57 @@
 BF16 = jnp.bfloat16
 
 
+OWN = -1
+
+
+def make_source():
+    source = {}
+    for way in range(4):
+        first, part = way // 2, way % 2
+        across = (2, 3) if first == 0 else (0, 1)
+        for k in range(2):
+            source[way, k] = (OWN, first, k)
+            source[way, 2 + k] = (OWN, 1 - first, k)
+        source[way, 4] = (way, part)
+        source[way, 5] = (across[0], 0)
+        source[way, 6] = (across[1], 0)
+        source[way, 7] = (across[0], 1)
+        source[way, 8] = (across[1], 1)
+        source[way, 9] = (way, 2 + part)
+        source[way, 10] = (across[0], 4)
+        source[way, 11] = (across[1], 4)
+        source[way, 12] = (way, 7 if part else 5)
+        source[way, 13] = (way, 8 if part else 6)
+        source[way, 14] = (way, 11 if part else 10)
+    return source
+
+
+SOURCE = make_source()
+
+
+def children(slot):
+    return [key for key, value in sorted(SOURCE.items(), key=lambda item: item[0][1]) if value == slot]
+
+
+def identity(slot):
+    if slot[0] == OWN:
+        return (0, 0, slot[1], slot[2])
+    dx, dy, half, part = identity(SOURCE[slot])
+    step = 1 if slot[0] % 2 else 3
+    if slot[0] < 2:
+        return ((dx + step) % 4, dy, half, part)
+    return (dx, (dy + step) % 4, half, part)
+
+
+def text_row(slot):
+    if slot[0] == OWN:
+        return 896 + 32 * slot[1] + 16 * slot[2]
+    way, tick = slot
+    if tick == 14:
+        return 960 + 16 * way
+    return 128 * (tick // 2) + 32 * way + 16 * (tick % 2)
+
+
 def dot_nn(a, b):
     return lax.dot_general(a, b, (((1,), (0,)), ((), ())), preferred_element_type=F32)
 
@@ -37,30 +88,27 @@
 def kernel(
     video_ref, text_ref, ids_ref, log_scale_ref, bias_ref,
     loss_ref, vgrad_ref, tgrad_ref,
-    vf, tf, vh, vl, th, tl, w, vg, tg, recv_t, recv_v, recv_s, ids_slot, ids_vec, vidx, lacc, lrow, lrecv, inv_v, inv_t,
+    vf, tf, vh, vl, th, tl, w, vg, tg, recv_t, recv_v, recv_s, ids_all, ids_vec, vidx, lacc, lrow, lrecv, inv_v, inv_t,
     t_send, t_recv, z_send, z_recv, s_send, s_recv, i_send, i_recv,
     rt_send, rt_recv, rz_send, rz_recv, rs_send, rs_recv, l_send, l_recv,
 ):
     row, col = lax.axis_index("row"), lax.axis_index("col")
     z, x, y, core = row // 4, row % 4, col // 2, col % 2
-    diag = (x + y) % 4
 
     def at(x_, y_, z_, core_):
         return (z_ * 4 + x_, y_ * 2 + core_)
 
     xp, xm, yp, ym = (x + 1) % 4, (x + 3) % 4, (y + 1) % 4, (y + 3) % 4
-    next_a = at(jnp.where(diag == 3, x, xp), jnp.where(diag == 3, yp, y), z, core)
-    next_b = at(jnp.where(diag == 3, xp, x), jnp.where(diag == 3, y, yp), z, core)
-    prev_a = at(jnp.where(diag == 0, x, xm), jnp.where(diag == 0, ym, y), z, core)
-    prev_b = at(jnp.where(diag == 0, xm, x), jnp.where(diag == 0, y, ym), z, core)
-    t_out = (next_a, prev_a, next_b, prev_b)
-    t_back = (prev_a, next_a, prev_b, next_b)
+    t_out = (at(xp, y, z, core), at(xm, y, z, core), at(x, yp, z, core), at(x, ym, z, core))
+    t_back = (t_out[1], t_out[0], t_out[3], t_out[2])
+    line_x = tuple(at((x + d) % 4, y, z, core) for d in range(4))
+    line_y = tuple(at(x, (y + d) % 4, z, core) for d in range(4))
     z_out = (at(x, y, (z + 1) % 8, core), at(x, y, (z + 7) % 8, core))
     z_back = (z_out[1], z_out[0])
     other = at(x, y, z, 1 - core)
 
     barrier = pltpu.get_barrier_semaphore()
-    for peer in t_out:
+    for peer in line_x[1:] + line_y[1:]:
         pl.semaphore_signal(barrier, inc=1, device_id=peer, device_id_type=MESH)
     pl.semaphore_signal(barrier, inc=1, device_id=other, device_id_type=MESH)
     for step in range(1, 8):
@@ -85,9 +133,10 @@
         vh[rows(768 + 128 * half, 32), :] = hi[32 * half : 32 * half + 32]
         vl[rows(768 + 128 * half, 32), :] = lo[32 * half : 32 * half + 32]
 
-    def t_copy(way, tick, src, dst):
-        return pltpu.make_async_remote_copy(
-            src_ref=tf.at[rows(src, 16)], dst_ref=tf.at[rows(dst, 16)],
+    def t_copy(slot):
+        way, tick = slot
+        return pltpu.make_async_remote_copy(
+            src_ref=tf.at[rows(text_row(SOURCE[slot]), 16)], dst_ref=tf.at[rows(text_row(slot), 16)],
             send_sem=t_send.at[way], recv_sem=t_recv.at[way, tick],
             device_id=t_out[way], device_id_type=MESH,
         )
@@ -106,23 +155,34 @@
             device_id=other, device_id_type=MESH,
         )
 
-    def i_copy(way, step, src):
-        return pltpu.make_async_remote_copy(
-            src_ref=src, dst_ref=ids_slot.at[way, step],
-            send_sem=i_send.at[way], recv_sem=i_recv.at[way, step],
-            device_id=t_out[way], device_id_type=MESH,
-        )
-
-    pl.semaphore_wait(barrier, 19)
-
-    for way in range(4):
-        i_copy(way, 0, ids_ref.at[way // 2]).start()
+    def ix_copy(d):
+        return pltpu.make_async_remote_copy(
+            src_ref=ids_ref, dst_ref=ids_all.at[0, (4 - d) % 4],
+            send_sem=i_send.at[0], recv_sem=i_recv.at[0, (4 - d) % 4],
+            device_id=line_x[d], device_id_type=MESH,
+        )
+
+    def iy_copy(d):
+        return pltpu.make_async_remote_copy(
+            src_ref=ids_all.at[0], dst_ref=ids_all.at[(4 - d) % 4],
+            send_sem=i_send.at[1], recv_sem=i_recv.at[1, (4 - d) % 4],
+            device_id=line_y[d], device_id_type=MESH,
+        )
+
+    pl.semaphore_wait(barrier, 21)
+
+    for d in range(1, 4):
+        ix_copy(d).start()
+    ids_all[0, 0] = ids_ref[...]
     for part in range(2):
         for way in range(4):
-            t_copy(way, part, 896 + 32 * (way // 2) + 16 * part, 32 * way + 16 * part).start()
+            t_copy((way, part)).start()
         for way in range(2):
             for q in (2 * part, 2 * part + 1):
                 z_copy(way, q, 768 + 128 * (q // 2) + 16 * (q % 2), 128 * (q // 2) + 64 * way + 16 * (q % 2)).start()
+    for k in range(2, 4):
+        for way in range(4):
+            t_copy((way, k)).start()
     for q in range(4):
         s_copy(q // 2, 14 + q % 2, 768 + 128 * (q // 2) + 16 * (q % 2)).start()
 
@@ -182,6 +242,20 @@
                 w[vb * 2 + k, 1, :, cols] = lo[128 * k : 128 * k + 128]
         lacc[vs, :] += total
 
+    def group_ids(group):
+        vec = jnp.zeros((1, 128), jnp.int32)
+        for place in range(8):
+            if group < 7:
+                slot = (place // 2, 2 * group + place % 2)
+            elif place < 4:
+                slot = (OWN, place // 2, place % 2)
+            else:
+                slot = (place - 4, 14)
+            dx, dy, half, part = identity(slot)
+            ids = ids_all[dy, dx, pl.ds(2 * half + part, 1), :]
+            vec = ids if place == 0 else jnp.where(lane < 16 * place, vec, ids)
+        return vec
+
     def count(tick):
         done = 0
         for bound, more in ((4, 1), (8, 1), (9, 1), (10, 1), (12, 2), (13, 2), (14, 8)):
@@ -190,57 +264,26 @@
 
     @pl.loop(0, 15)
     def _(tick):
-        part = tick % 2
-        step = tick // 2
-        base = 128 * step + 16 * part
-
-        @pl.when(tick < 14)
-        def _():
-            for way in range(4):
-                slot = base + 32 * way
-                t_copy(way, tick, slot, slot).wait_recv()
-
-                @pl.when(tick < 12)
-                def _():
-                    t_copy(way, tick + 2, slot, slot + 128).start()
-
-                @pl.when((tick >= 12) & (part == way % 2))
-                def _():
-                    t_copy(way, 14, slot, 960 + 32 * (way // 2) + 16 * (way % 2)).start()
-
-            @pl.when(part == 0)
+        base = 128 * (tick // 2) + 16 * (tick % 2)
+
+        for k in range(15):
+
+            @pl.when(tick == k)
             def _():
                 for way in range(4):
-                    i_copy(way, step, ids_slot.at[way, step]).wait_recv()
-
-                    @pl.when(tick < 12)
-                    def _():
-                        i_copy(way, step + 1, ids_slot.at[way, step]).start()
-
-                    if way % 2 == 0:
-
-                        @pl.when(tick == 12)
-                        def _():
-                            i_copy(way, 7, ids_slot.at[way, step]).start()
-
-                ids_vec[step] = jnp.where(
-                    lane < 64,
-                    jnp.where(lane < 32, ids_slot[0, step], ids_slot[1, step]),
-                    jnp.where(lane < 96, ids_slot[2, step], ids_slot[3, step]),
-                )
-
-        @pl.when(tick == 14)
-        def _():
-            for way in range(4):
-                slot = 960 + 32 * (way // 2) + 16 * (way % 2)
-                t_copy(way, 14, slot, slot).wait_recv()
-            for way in (0, 2):
-                i_copy(way, 7, ids_slot.at[way, 7]).wait_recv()
-            ids_vec[7] = jnp.where(
-                lane < 64,
-                jnp.where(lane < 32, ids_ref[0], ids_ref[1]),
-                jnp.where(lane < 96, ids_slot[0, 7], ids_slot[2, 7]),
-            )
+                    t_copy((way, k)).wait_recv()
+                    for child in children((way, k)):
+                        t_copy(child).start()
+                if k == 0:
+                    for d in range(1, 4):
+                        ix_copy(d).wait_recv()
+                    for d in range(1, 4):
+                        iy_copy(d).start()
+                if k == 3:
+                    for d in range(1, 4):
+                        iy_copy(d).wait_recv()
+                    for group in range(8):
+                        ids_vec[group] = group_ids(group)
 
         for way in range(2):
 
@@ -306,23 +349,28 @@
         def _(n):
             block(n)
 
-    def rt_copy(way, part, step, src, dst):
-        return pltpu.make_async_remote_copy(
-            src_ref=tg.at[rows(src, 16)], dst_ref=recv_t.at[rows(dst, 16)],
-            send_sem=rt_send.at[way], recv_sem=rt_recv.at[way, part, step],
+    def rt_copy(slot):
+        way, tick = slot
+        row_ = text_row(slot)
+        return pltpu.make_async_remote_copy(
+            src_ref=tg.at[rows(row_, 16)], dst_ref=recv_t.at[rows(row_, 16)],
+            send_sem=rt_send.at[way], recv_sem=rt_recv.at[way, tick],
             device_id=t_back[way], device_id_type=MESH,
         )
 
-    def rt_slot(way, part, step):
-        return jnp.where(step == 0, 896, 128 * (step - 1)) + 32 * way + 16 * part
-
-    def t_pump(step, part, first):
+    def t_sum(slot):
+        total = tg[rows(text_row(slot), 16), :]
+        for child in children(slot):
+            rt_copy(child).wait_recv()
+            total = total + recv_t[rows(text_row(child), 16), :]
+        return total
+
+    def t_pump(tick):
         for way in range(4):
-            slot = 128 * (step - 1) + 32 * way + 16 * part
-            if not first or way % 2 == part:
-                rt_copy(way, part, step, slot, slot).wait_recv()
-                tg[rows(slot, 16), :] += recv_t[rows(slot, 16), :]
-            rt_copy(way, part, step - 1, slot, rt_slot(way, part, step - 1)).start()
+            slot = (way, tick)
+            if children(slot):
+                tg[rows(text_row(slot), 16), :] = t_sum(slot)
+            rt_copy(slot).start()
 
     def rz_copy(way, half, step, src):
         return pltpu.make_async_remote_copy(
@@ -392,21 +440,15 @@
     def _(i):
         t_grad(7 - i)
 
-        @pl.when(i == 0)
-        def _():
-            for way in range(4):
-                part = way % 2
-                src = 960 + 32 * (way // 2) + 16 * part
-                rt_copy(way, part, 7, src, 768 + 32 * way + 16 * part).start()
+        for k in range(8):
+
+            @pl.when(i == k)
+            def _():
+                t_pump(14 if k == 0 else 15 - 2 * k)
 
         @pl.when(i == 1)
         def _():
-            t_pump(7, 0, True)
             z_last(0)
-
-        @pl.when(i >= 2)
-        def _():
-            t_pump(8 - i, 0, False)
 
         @pl.when(i == 2)
         def _():
@@ -429,13 +471,11 @@
         for way in range(2):
             rs_copy(hg, half, way).start()
 
-        @pl.when(i == 1)
-        def _():
-            t_pump(7, 1, True)
-
-        @pl.when(i >= 2)
-        def _():
-            t_pump(8 - i, 1, False)
+        for k in range(1, 8):
+
+            @pl.when(i == k)
+            def _():
+                t_pump(14 - 2 * k)
 
         @pl.when(i == 3)
         def _():
@@ -454,16 +494,12 @@
         loss = loss + lrecv[(hg * 2 + way) * 2 + who][:, first : first + 32]
     loss_ref[...] = loss
 
-    for ring in range(2):
+    for half in range(2):
         for part in range(2):
-            own = 896 + 32 * ring + 16 * part
-            total = tg[rows(own, 16), :]
-            for way in (2 * ring, 2 * ring + 1):
-                slot = 896 + 32 * way + 16 * part
-                rt_copy(way, part, 0, own, slot).wait_recv()
-                total = total + recv_t[rows(slot, 16), :]
+            own = text_row((OWN, half, part))
+            total = t_sum((OWN, half, part))
             u = tf[rows(own, 16), :]
-            first = 32 * ring + 16 * part
+            first = 32 * half + 16 * part
             back = total - u * jnp.sum(u * total, axis=1, keepdims=True)
             tgrad_ref[rows(first, 16), :] = back * inv_t[rows(first, 16), :1]
 
@@ -486,17 +522,18 @@
     for way in range(4):
         drain(tf.at[rows(0, 240)], t_send.at[way])
         drain(tg.at[rows(0, 240)], rt_send.at[way])
-        drain(ids_slot.at[way, pl.ds(0, 8 if way % 2 == 0 else 7)], i_send.at[way])
     for way in range(2):
         drain(vf.at[rows(0, 224)], z_send.at[way])
         drain(vf.at[rows(0, 256)], s_send.at[way])
         drain(vg.at[rows(0, 224)], rz_send.at[way])
+    drain(ids_all.at[0, pl.ds(0, 3)], i_send.at[0])
+    drain(ids_all.at[pl.ds(0, 3)], i_send.at[1])
     drain(vg.at[rows(0, 512)], rs_send.at[0])
     drain(lrecv.at[pl.ds(0, 15)], l_send.at[0])
 
 
 def shards(video, text, match_ids, log_scale, bias):
-    ids = jnp.tile(match_ids.reshape(2, 1, 32), (1, 1, 4))
+    ids = jnp.tile(match_ids.reshape(4, 16), (1, 8))
     vmem = pl.BlockSpec(memory_space=pltpu.VMEM)
     smem = pl.BlockSpec(memory_space=pltpu.SMEM)
     dma = pltpu.SemaphoreType.DMA
@@ -522,7 +559,7 @@
             pltpu.VMEM((1024, 1024), F32),
             pltpu.VMEM((4, 2, 2, 32, 1024), F32),
             pltpu.VMEM((4, 2, 2, 32, 1024), F32),
-            pltpu.VMEM((4, 8, 1, 128), jnp.int32),
+            pltpu.VMEM((4, 4, 4, 128), jnp.int32),
             pltpu.VMEM((8, 1, 128), jnp.int32),
             pltpu.VMEM((1024, 128), jnp.int32),
             pltpu.VMEM((1024, 128), F32),
@@ -533,8 +570,8 @@
             dma((4,)), dma((4, 15)),
             dma((2,)), dma((2, 14)),
             dma((2,)), dma((2, 16)),
-            dma((4,)), dma((4, 8)),
-            dma((4,)), dma((4, 2, 8)),
+            dma((2,)), dma((2, 4)),
+            dma((4,)), dma((4, 15)),
             dma((2,)), dma((2, 2, 4)),
             dma((1,)), dma((4, 2, 2)),
             dma((1,)), dma((16,)),

time: 100 us -> 85.5 us (0.85)
  Pallas kernels: 93.6 us -> 79 us
    pallas_call x1, Pallas kernels: 93.6 us -> 79 us  [shards(): pl.pallas_call(kernel, out_shape=(jax.ShapeDtypeStruct((2, 32), F32), jax...]
where the time goes in v2:
time: 85.5 us; the launch traced here: 85.4 us
  Pallas kernels  79 us (92%)
  local copies, waits for them, and re-layouts  4.42 us (5%)
  between operations  1.97 us (2%)
    pallas_call x1, Pallas kernels, shards(): pl.pallas_call(kernel, out_shape=(jax.ShapeDtypeStruct((2, 32), F32), jax...  79 us
    unnamed x8, local copies, waits for them, and re-layouts  3.08 us

profile of v2, /device:TPU:1, one launch (start us, length us, event | category | flops | bytes accessed | tf_op | source)
XLA Modules:
  0.0 85.4 jit_solution(1160728551168691817)
XLA Ops:
  1.3 0.0 copy-start.1
  1.9 0.0 copy-done.1
  2.0 0.1 tile.10
  2.0 0.7 tile.12.ids_ref
  2.7 79.0 %shard_map.76 = (f32[2,32]{1,0:T(2,128)}, f32[64,1024]{1,0:T(8,128)}, f32[64,1024]{1,0:T(8,128)}) custom-call(f32[64,1024]{1,0:T(8,128)} %video_ref.1, f32[64,1024]{1,0:T(8,128)} %text_ref.1, s32[4,128]{1,0:T(4,128)} %tile.12.ids_ref, f32[1]{0:T(128)S(6)} %copy.10.log_scale_ref, f32[1]{0:T(128)S(6)} %copy.11.bias_ref), custom_call_target="tpu_custom_call" | custom-call | flops 19327352832 | bytes 1048576 | tf_op jit(solution)/shard_map/pallas_call | solution.py:540
  81.7 0.0 copy-start.2
  81.7 0.7 copy-done.2
  82.4 0.6 reshape.13
  82.9 0.0 copy-start
  82.9 1.7 %copy.12 = f32[64,1024]{1,0:T(8,128)} copy(f32[64,1024]{1,0:T(8,128)} %get-tuple-element.13) | data formatting | bytes 524288
  84.7 0.0 copy-done
  84.7 0.7 copy.13
  (1 shorter events, 0.0 us)
Async XLA Ops:
  1.3 0.7 copy-start.1
  81.7 0.7 copy-start.2
  82.9 1.7 %copy-start = (f32[64,1024]{1,0:T(8,128)S(1)}, f32[64,1024]{1,0:T(8,128)}, u32[]{:S(2)}) copy-start(f32[64,1024]{1,0:T(8,128)} %get-tuple-element.14) | copy-start | bytes 786436

commit v3 on v2

--- a/solution.py
+++ b/solution.py
@@ -9,6 +9,7 @@
 MESH = pl.DeviceIdType.MESH
 F32 = jnp.float32
 BF16 = jnp.bfloat16
+F8 = jnp.float8_e4m3fn
 
 
 OWN = -1
@@ -53,6 +54,12 @@
     return (dx, (dy + step) % 4, half, part)
 
 
+def video_row(hg, half, way, who):
+    if isinstance(hg, int) and hg == 3:
+        return 768 + 128 * way + 64 * half + 32 * who
+    return 256 * hg + 128 * half + 64 * way + 32 * who
+
+
 def text_row(slot):
     if slot[0] == OWN:
         return 896 + 32 * slot[1] + 16 * slot[2]
@@ -76,7 +83,11 @@
 
 def split(x):
     hi = x.astype(BF16)
-    return hi, (x - hi.astype(F32)).astype(BF16)
+    return hi, x - hi.astype(F32)
+
+
+HI8, LO8 = 2.0**8, 2.0**17
+W_HI8, W_LO8 = 2.0**4, 2.0**13
 
 
 def rows(start, size):
@@ -86,11 +97,11 @@
 
 
 def kernel(
-    video_ref, text_ref, ids_ref, log_scale_ref, bias_ref,
+    video_any, text_any, ids_any, log_scale_any, bias_any,
     loss_ref, vgrad_ref, tgrad_ref,
-    vf, tf, vh, vl, th, tl, w, vg, tg, recv_t, recv_v, recv_s, ids_all, ids_vec, vidx, lacc, lrow, lrecv, inv_v, inv_t,
+    vf, tf, vh, v8, th, t8, dots, w, w8, vg, tg, recv_t, recv_v, recv_s, ids_all, ids_own, ids_vec, vidx, lacc, lrow, lrecv, inv_v, inv_t, video_ref, text_ref, ids_ref, log_scale_ref, bias_ref,
     t_send, t_recv, z_send, z_recv, s_send, s_recv, i_send, i_recv,
-    rt_send, rt_recv, rz_send, rz_recv, rs_send, rs_recv, l_send, l_recv,
+    rt_send, rt_recv, rz_send, rz_recv, rs_send, rs_recv, l_send, l_recv, in_sem,
 ):
     row, col = lax.axis_index("row"), lax.axis_index("col")
     z, x, y, core = row // 4, row % 4, col // 2, col % 2
@@ -107,6 +118,18 @@
     z_back = (z_out[1], z_out[0])
     other = at(x, y, z, 1 - core)
 
+    loads = [
+        pltpu.make_async_copy(src, dst, in_sem.at[n])
+        for n, (src, dst) in enumerate(
+            (
+                (text_any, text_ref), (video_any, video_ref), (ids_any, ids_ref),
+                (log_scale_any, log_scale_ref), (bias_any, bias_ref),
+            )
+        )
+    ]
+    for load in loads:
+        load.start()
+
     barrier = pltpu.get_barrier_semaphore()
     for peer in line_x[1:] + line_y[1:]:
         pl.semaphore_signal(barrier, inc=1, device_id=peer, device_id_type=MESH)
@@ -121,17 +144,20 @@
         inv_ref[...] = jnp.broadcast_to(inv, (64, 128))
         return full * inv
 
+    loads[0].wait()
     tu = unit(text_ref, inv_t)
     tf[rows(896, 64), :] = tu
-    hi, lo = split(tu)
-    th[rows(896, 64), :] = hi
-    tl[rows(896, 64), :] = lo
+    loads[1].wait()
     vu = unit(video_ref, inv_v)
-    hi, lo = split(vu)
     for half in range(2):
-        vf[rows(768 + 128 * half, 32), :] = vu[32 * half : 32 * half + 32]
-        vh[rows(768 + 128 * half, 32), :] = hi[32 * half : 32 * half + 32]
-        vl[rows(768 + 128 * half, 32), :] = lo[32 * half : 32 * half + 32]
+        vf[rows(768 + 64 * half, 32), :] = vu[32 * half : 32 * half + 32]
+    lane = lax.broadcasted_iota(jnp.int32, (1, 128), 1)
+    loads[2].wait()
+    for quarter in range(4):
+        vec = jnp.zeros((1, 128), jnp.int32)
+        for n in range(16):
+            vec = jnp.where(lane % 16 == n, ids_ref[16 * quarter + n], vec)
+        ids_own[quarter : quarter + 1, :] = vec
 
     def t_copy(slot):
         way, tick = slot
@@ -157,7 +183,7 @@
 
     def ix_copy(d):
         return pltpu.make_async_remote_copy(
-            src_ref=ids_ref, dst_ref=ids_all.at[0, (4 - d) % 4],
+            src_ref=ids_own, dst_ref=ids_all.at[0, (4 - d) % 4],
             send_sem=i_send.at[0], recv_sem=i_recv.at[0, (4 - d) % 4],
             device_id=line_x[d], device_id_type=MESH,
         )
@@ -173,18 +199,18 @@
 
     for d in range(1, 4):
         ix_copy(d).start()
-    ids_all[0, 0] = ids_ref[...]
+    ids_all[0, 0] = ids_own[...]
     for part in range(2):
         for way in range(4):
             t_copy((way, part)).start()
         for way in range(2):
             for q in (2 * part, 2 * part + 1):
-                z_copy(way, q, 768 + 128 * (q // 2) + 16 * (q % 2), 128 * (q // 2) + 64 * way + 16 * (q % 2)).start()
+                z_copy(way, q, 768 + 64 * (q // 2) + 16 * (q % 2), 128 * (q // 2) + 64 * way + 16 * (q % 2)).start()
     for k in range(2, 4):
         for way in range(4):
             t_copy((way, k)).start()
     for q in range(4):
-        s_copy(q // 2, 14 + q % 2, 768 + 128 * (q // 2) + 16 * (q % 2)).start()
+        s_copy(q // 2, 14 + q % 2, 768 + 64 * (q // 2) + 16 * (q % 2)).start()
 
     local = lax.broadcasted_iota(jnp.int32, (32, 128), 0)
     for hg in range(4):
@@ -197,34 +223,52 @@
                         from_z = (z + 4 * way) % 8
                     from_core = core if who == 0 else 1 - core
                     base = ((from_z * 4 + x) * 8 + y * 2 + from_core) * 64 + 32 * half
-                    vidx[rows(256 * hg + 128 * half + 64 * way + 32 * who, 32), :] = local + base
+                    vidx[rows(video_row(hg, half, way, who), 32), :] = local + base
     lacc[...] = jnp.zeros_like(lacc)
 
+    loads[3].wait()
+    loads[4].wait()
     scale = jnp.exp(jnp.full((1, 128), log_scale_ref[0], F32))
     bias = jnp.full((1, 128), bias_ref[0], F32)
-    lane = lax.broadcasted_iota(jnp.int32, (1, 128), 1)
 
     def t_split(start, size):
-        hi, lo = split(tf[rows(start, size), :])
+        full = tf[rows(start, size), :]
+        hi, lo = split(full)
         th[rows(start, size), :] = hi
-        tl[rows(start, size), :] = lo
+        t8[0, rows(start, size), :] = (lo * LO8).astype(F8)
+        t8[1, rows(start, size), :] = (full * HI8).astype(F8)
 
     def v_split(start, size):
-        hi, lo = split(vf[rows(start, size), :])
+        full = vf[rows(start, size), :]
+        hi, lo = split(full)
         vh[rows(start, size), :] = hi
-        vl[rows(start, size), :] = lo
+        v8[0, rows(start, size), :] = (full * HI8).astype(F8)
+        v8[1, rows(start, size), :] = (lo * LO8).astype(F8)
 
     def v_slot(tick, way):
         q = tick % 4
         return 256 * (tick // 4) + 128 * (q // 2) + 64 * way + 16 * (q % 2)
 
-    def block(n):
+    def place(n):
+        if isinstance(n, int):
+            m = int(n**0.5)
+            r = n - m * m
+            return (r, m) if r <= m else (m, r - m - 1)
         m = (n >= 1).astype(jnp.int32) + (n >= 4).astype(jnp.int32) + (n >= 9).astype(jnp.int32)
         r = n - m * m
-        vb = jnp.where(r <= m, r, m)
-        tb = jnp.where(r <= m, m, r - m - 1)
+        return jnp.where(r <= m, r, m), jnp.where(r <= m, m, r - m - 1)
+
+    def block_dots(n):
+        vb, tb = place(n)
         vs, ts = rows(vb * 256, 256), rows(tb * 256, 256)
-        dots = dot_nt(vh[vs, :], th[ts, :]) + (dot_nt(vh[vs, :], tl[ts, :]) + dot_nt(vl[vs, :], th[ts, :]))
+        small = dot_nt(
+            jnp.concatenate([v8[0, vs, :], v8[1, vs, :]], axis=1), jnp.concatenate([t8[0, ts, :], t8[1, ts, :]], axis=1)
+        )
+        dots[...] = dot_nt(vh[vs, :], th[ts, :]) + small * (1.0 / (HI8 * LO8))
+
+    def block_rest(n):
+        vb, tb = place(n)
+        vs = rows(vb * 256, 256)
         total = jnp.zeros((256, 128), F32)
         for half in range(2):
             logits = dots[:, 128 * half : 128 * half + 128] * scale + bias
@@ -236,24 +280,26 @@
             small = e * (1.0 - e * (0.5 - e * (1.0 / 3.0)))
             total = total + jnp.where(e < 1.0 / 64.0, small, jnp.log(u))
             hi, lo = split(weight)
-            cols = pl.ds(pl.multiple_of((tb * 2 + half) * 128, 128), 128)
+            hi8, lo8 = (weight * W_HI8).astype(F8), (lo * W_LO8).astype(F8)
+            cols = rows((tb * 2 + half) * 128, 128)
             for k in range(2):
-                w[vb * 2 + k, 0, :, cols] = hi[128 * k : 128 * k + 128]
-                w[vb * 2 + k, 1, :, cols] = lo[128 * k : 128 * k + 128]
+                w[vb * 2 + k, :, cols] = hi[128 * k : 128 * k + 128]
+                w8[0, vb * 2 + k, :, cols] = hi8[128 * k : 128 * k + 128]
+                w8[1, vb * 2 + k, :, cols] = lo8[128 * k : 128 * k + 128]
         lacc[vs, :] += total
 
     def group_ids(group):
         vec = jnp.zeros((1, 128), jnp.int32)
-        for place in range(8):
+        for spot in range(8):
             if group < 7:
-                slot = (place // 2, 2 * group + place % 2)
-            elif place < 4:
-                slot = (OWN, place // 2, place % 2)
+                slot = (spot // 2, 2 * group + spot % 2)
+            elif spot < 4:
+                slot = (OWN, spot // 2, spot % 2)
             else:
-                slot = (place - 4, 14)
+                slot = (spot - 4, 14)
             dx, dy, half, part = identity(slot)
             ids = ids_all[dy, dx, pl.ds(2 * half + part, 1), :]
-            vec = ids if place == 0 else jnp.where(lane < 16 * place, vec, ids)
+            vec = ids if spot == 0 else jnp.where(lane < 16 * spot, vec, ids)
         return vec
 
     def count(tick):
@@ -264,8 +310,6 @@
 
     @pl.loop(0, 15)
     def _(tick):
-        base = 128 * (tick // 2) + 16 * (tick % 2)
-
         for k in range(15):
 
             @pl.when(tick == k)
@@ -298,56 +342,61 @@
 
                 @pl.when((tick >= 8) & ((tick % 4) // 2 == way))
                 def _():
-                    last = 768 + 128 * way + 64 + 16 * (tick % 2)
+                    last = 896 + 64 * way + 16 * (tick % 2)
                     z_copy(way, 12 + tick % 2, slot, last).start()
 
                 s_copy(way, tick, slot).start()
 
             @pl.when((tick == 12) | (tick == 13))
             def _():
-                slot = 768 + 128 * way + 64 + 16 * (tick % 2)
+                slot = 896 + 64 * way + 16 * (tick % 2)
                 z_copy(way, tick, slot, slot).wait_recv()
                 s_copy(way, tick, slot).start()
 
             @pl.when((tick >= 1) & (tick <= 12))
             def _():
-                slot = v_slot(tick - 1, way)
-                s_copy(way, tick - 1, slot).wait_recv()
-                v_split(slot + 32, 16)
+                s_copy(way, tick - 1, v_slot(tick - 1, way)).wait_recv()
 
             @pl.when(tick >= 13)
             def _():
-                slot = 768 + 128 * way + 64 + 16 * ((tick - 1) % 2)
-                s_copy(way, tick - 1, slot).wait_recv()
-                v_split(slot + 32, 16)
-
-            @pl.when(tick < 12)
+                s_copy(way, tick - 1, 896 + 64 * way + 16 * ((tick - 1) % 2)).wait_recv()
+
+            @pl.when(tick == 1)
             def _():
-                v_split(v_slot(tick, way), 16)
-
-            @pl.when((tick == 12) | (tick == 13))
-            def _():
-                v_split(768 + 128 * way + 64 + 16 * (tick % 2), 16)
-
-            @pl.when(tick == 0)
-            def _():
-                for part_ in range(2):
-                    slot = 768 + 128 * way + 16 * part_
-                    s_copy(way, 14 + part_, slot).wait_recv()
-                    v_split(slot + 32, 16)
-
-        @pl.when(tick < 14)
-        def _():
-            for way in range(4):
-                t_split(base + 32 * way, 16)
+                for part in range(2):
+                    s_copy(way, 14 + part, 768 + 64 * way + 16 * part).wait_recv()
+
+        @pl.when(tick == 0)
+        def _():
+            t_split(896, 64)
+
+        @pl.when(tick % 2 == 1)
+        def _():
+            t_split(128 * (tick // 2), 128)
+
+        @pl.when((tick % 2 == 0) & (tick >= 2) & (tick <= 12))
+        def _():
+            v_split(128 * (tick // 2 - 1), 128)
+
+        @pl.when(tick == 1)
+        def _():
+            v_split(768, 128)
 
         @pl.when(tick == 14)
         def _():
+            v_split(896, 128)
             t_split(960, 64)
 
-        @pl.loop(count(tick - 1), count(tick))
+        @pl.when(tick == 4)
+        def _():
+            block_dots(0)
+
+        @pl.loop(jnp.maximum(count(tick - 1), 1), count(tick))
         def _(n):
-            block(n)
+            block_rest(n - 1)
+            block_dots(n)
+
+    block_rest(15)
 
     def rt_copy(slot):
         way, tick = slot
@@ -380,9 +429,8 @@
         )
 
     def rs_copy(hg, half, way):
-        src = 256 * hg + 128 * half + 64 * way + 32
-        return pltpu.make_async_remote_copy(
-            src_ref=vg.at[rows(src, 32)], dst_ref=recv_s.at[hg, half, way],
+        return pltpu.make_async_remote_copy(
+            src_ref=vg.at[rows(video_row(hg, half, way, 1), 32)], dst_ref=recv_s.at[hg, half, way],
             send_sem=rs_send.at[0], recv_sem=rs_recv.at[hg, half, way],
             device_id=other, device_id_type=MESH,
         )
@@ -398,22 +446,24 @@
                 vg[rows(slot, 32), :] += recv_s[hg, half, way]
             rz_copy(way, half, hg, slot).start()
 
-    def z_last(half):
-        slot = 768 + 128 * half + 64
-        rs_copy(3, half, 1).wait_recv()
-        vg[rows(slot, 32), :] += recv_s[3, half, 1]
-        rz_copy(half, half, 3, slot).start()
+    def z_last():
+        for half in range(2):
+            slot = 896 + 64 * half
+            rs_copy(3, half, 1).wait_recv()
+            vg[rows(slot, 32), :] += recv_s[3, half, 1]
+            rz_copy(half, half, 3, slot).start()
 
     def t_grad(g):
         cols = pl.ds(pl.multiple_of(g * 128, 128), 128)
-        hi = w[:, 0, :, cols].reshape(1024, 128)
-        lo = w[:, 1, :, cols].reshape(1024, 128)
-        both = dot_tn(jnp.concatenate([hi, lo], axis=1), vh[...])
-        tg[rows(g * 128, 128), :] = both[:128] + (both[128:] + dot_tn(hi, vl[...]))
+        hi = w[:, :, cols].reshape(1024, 128)
+        lo8 = w8[1, :, :, cols].reshape(1024, 128)
+        hi8 = w8[0, :, :, cols].reshape(1024, 128)
+        small = dot_tn(jnp.concatenate([lo8, hi8], axis=0), v8[...].reshape(2048, 1024))
+        tg[rows(g * 128, 128), :] = dot_tn(hi, vh[...]) + small * (1.0 / (W_HI8 * LO8))
 
     def v_grad(m):
-        both = dot_nn(w[m].reshape(256, 1024), th[...])
-        vg[rows(m * 128, 128), :] = both[:128] + (both[128:] + dot_nn(w[m, 0], tl[...]))
+        small = dot_nn(jnp.concatenate([w8[0, m], w8[1, m]], axis=1), t8[...].reshape(2048, 1024))
+        vg[rows(m * 128, 128), :] = dot_nn(w[m], th[...]) + small * (1.0 / (W_HI8 * LO8))
 
     def l_copy(hg, way, who, owner):
         slot = (hg * 2 + way) * 2 + who
@@ -436,46 +486,47 @@
                         peers.append((hg, way, who, at(x, y, to_z, core if who == 0 else 1 - core)))
         return peers
 
-    @pl.loop(0, 8)
+    t_grad(7)
+    t_pump(14)
+
+    @pl.loop(0, 7)
     def _(i):
-        t_grad(7 - i)
-
-        for k in range(8):
+        hg, half = 2 - (i - 1) // 2, (i - 1) % 2
+        v_grad(jnp.where(i == 0, 7, 2 * hg + half))
+
+        @pl.when(i == 0)
+        def _():
+            for half_ in range(2):
+                rs_copy(3, half_, 1).start()
+
+        @pl.when(i > 0)
+        def _():
+            for way in range(2):
+                rs_copy(hg, half, way).start()
+
+        t_grad(6 - i)
+        for k in range(7):
 
             @pl.when(i == k)
             def _():
-                t_pump(14 if k == 0 else 15 - 2 * k)
+                t_pump(13 - 2 * k)
+                t_pump(12 - 2 * k)
+
+        @pl.when(i == 0)
+        def _():
+            z_last()
 
         @pl.when(i == 1)
         def _():
-            z_last(0)
+            z_pump(2, 0, (True, False))
 
         @pl.when(i == 2)
         def _():
-            z_last(1)
-
-        @pl.when(i == 3)
-        def _():
-            z_pump(2, 0, (True, False))
-
-        @pl.when(i == 4)
-        def _():
             z_pump(2, 1, (False, True))
 
-        @pl.when(i >= 5)
-        def _():
-            z_pump(2 - (i - 3) // 2, (i - 3) % 2, (True, True))
-
-        hg, half = 3 - i // 2, i % 2
-        v_grad(2 * hg + half)
-        for way in range(2):
-            rs_copy(hg, half, way).start()
-
-        for k in range(1, 8):
-
-            @pl.when(i == k)
-            def _():
-                t_pump(14 - 2 * k)
+        @pl.when(i >= 3)
+        def _():
+            z_pump(hg, half, (True, True))
 
         @pl.when(i == 3)
         def _():
@@ -485,14 +536,23 @@
             for hg_, way, who, owner in l_peers():
                 l_copy(hg_, way, who, owner).start()
 
-    z_pump(0, 1, (True, True))
-
-    loss = lrow[3][:, :32]
+    v_grad(6)
+    for half in range(2):
+        rs_copy(3, half, 0).start()
+
+    loss = [lrow[3, 0:1, 64 * half : 64 * half + 32] for half in range(2)]
     for hg, way, who, owner in l_peers():
         l_copy(hg, way, who, owner).wait_recv()
-        first = 64 * way + 32 * who
-        loss = loss + lrecv[(hg * 2 + way) * 2 + who][:, first : first + 32]
-    loss_ref[...] = loss
+        part = lrecv.at[(hg * 2 + way) * 2 + who]
+        for half in range(2):
+            if hg < 3:
+                first = 64 * way + 32 * who
+                loss[half] = loss[half] + part[half : half + 1, first : first + 32]
+            else:
+                first = 64 * half + 32 * who
+                loss[half] = loss[half] + part[way : way + 1, first : first + 32]
+    loss_ref[:, :32] = loss[0]
+    loss_ref[:, 32:] = loss[1]
 
     for half in range(2):
         for part in range(2):
@@ -504,7 +564,7 @@
             tgrad_ref[rows(first, 16), :] = back * inv_t[rows(first, 16), :1]
 
     for half in range(2):
-        own = 768 + 128 * half
+        own = 768 + 64 * half
         rs_copy(3, half, 0).wait_recv()
         total = vg[rows(own, 32), :] + recv_s[3, half, 0]
         for way in range(2):
@@ -532,34 +592,42 @@
     drain(lrecv.at[pl.ds(0, 15)], l_send.at[0])
 
 
+def hand_on(loss_ref, vgrad_ref, tgrad_ref, loss_out, vgrad_out, tgrad_out):
+    loss_out[...] = loss_ref[...]
+    vgrad_out[...] = vgrad_ref[...]
+    tgrad_out[...] = tgrad_ref[...]
+
+
 def shards(video, text, match_ids, log_scale, bias):
-    ids = jnp.tile(match_ids.reshape(4, 16), (1, 8))
     vmem = pl.BlockSpec(memory_space=pltpu.VMEM)
-    smem = pl.BlockSpec(memory_space=pltpu.SMEM)
+    hbm = pl.BlockSpec(memory_space=pl.ANY)
     dma = pltpu.SemaphoreType.DMA
     loss, vgrad, tgrad = pl.pallas_call(
         kernel,
         out_shape=(
-            jax.ShapeDtypeStruct((2, 32), F32),
+            jax.ShapeDtypeStruct((1, 64), F32),
             jax.ShapeDtypeStruct((64, 1024), F32),
             jax.ShapeDtypeStruct((64, 1024), F32),
         ),
-        in_specs=[vmem, vmem, vmem, smem, smem],
+        in_specs=[hbm] * 5,
         out_specs=(vmem, vmem, vmem),
         scratch_shapes=[
             pltpu.VMEM((1024, 1024), F32),
             pltpu.VMEM((1024, 1024), F32),
             pltpu.VMEM((1024, 1024), BF16),
+            pltpu.VMEM((2, 1024, 1024), F8),
             pltpu.VMEM((1024, 1024), BF16),
-            pltpu.VMEM((1024, 1024), BF16),
-            pltpu.VMEM((1024, 1024), BF16),
-            pltpu.VMEM((8, 2, 128, 1024), BF16),
+            pltpu.VMEM((2, 1024, 1024), F8),
+            pltpu.VMEM((256, 256), F32),
+            pltpu.VMEM((8, 128, 1024), BF16),
+            pltpu.VMEM((2, 8, 128, 1024), F8),
             pltpu.VMEM((1024, 1024), F32),
             pltpu.VMEM((1024, 1024), F32),
             pltpu.VMEM((1024, 1024), F32),
             pltpu.VMEM((4, 2, 2, 32, 1024), F32),
             pltpu.VMEM((4, 2, 2, 32, 1024), F32),
             pltpu.VMEM((4, 4, 4, 128), jnp.int32),
+            pltpu.VMEM((4, 128), jnp.int32),
             pltpu.VMEM((8, 1, 128), jnp.int32),
             pltpu.VMEM((1024, 128), jnp.int32),
             pltpu.VMEM((1024, 128), F32),
@@ -567,6 +635,11 @@
             pltpu.VMEM((16, 2, 128), F32),
             pltpu.VMEM((64, 128), F32),
             pltpu.VMEM((64, 128), F32),
+            pltpu.VMEM((64, 1024), F32),
+            pltpu.VMEM((64, 1024), F32),
+            pltpu.SMEM((64,), jnp.int32),
+            pltpu.SMEM((1,), F32),
+            pltpu.SMEM((1,), F32),
             dma((4,)), dma((4, 15)),
             dma((2,)), dma((2, 14)),
             dma((2,)), dma((2, 16)),
@@ -574,13 +647,23 @@
             dma((4,)), dma((4, 15)),
             dma((2,)), dma((2, 2, 4)),
             dma((1,)), dma((4, 2, 2)),
-            dma((1,)), dma((16,)),
+            dma((1,)), dma((16,)), dma((5,)),
         ],
         compiler_params=pltpu.CompilerParams(
             collective_id=0, has_side_effects=True, vmem_limit_bytes=56 * 2**20
         ),
         cost_estimate=pl.CostEstimate(flops=18 * 2**30, bytes_accessed=2**20, transcendentals=3 * 2**20),
-    )(video, text, ids, log_scale, bias)
+    )(video, text, match_ids, log_scale, bias)
+    loss, vgrad, tgrad = pl.pallas_call(
+        hand_on,
+        out_shape=(
+            jax.ShapeDtypeStruct((1, 64), F32),
+            jax.ShapeDtypeStruct((64, 1024), F32),
+            jax.ShapeDtypeStruct((64, 1024), F32),
+        ),
+        in_specs=[vmem] * 3,
+        out_specs=(vmem,) * 3,
+    )(loss, vgrad, tgrad)
     return loss.reshape(64), vgrad, tgrad
 
 

time: 85.5 us -> 78.7 us (0.920)
  local copies, waits for them, and re-layouts: 4.42 us -> 0 us
  Pallas kernels: 79 us -> 76.7 us
    unnamed x8 -> x0, local copies, waits for them, and re-layouts: 3.08 us -> none
    pallas_call x1 -> x2, Pallas kernels: 79 us -> 76.7 us  [the longest x1 74.8 us: shards(): pl.pallas_call(kernel, out_shape=(jax.ShapeDtypeStruct((1, 64), F32), jax...]
where the time goes in v3:
time: 78.7 us; the launch traced here: 78.6 us
  Pallas kernels  76.7 us (97%)
  between operations  1.93 us (2%)
    pallas_call x1, Pallas kernels, shards(): pl.pallas_call(kernel, out_shape=(jax.ShapeDtypeStruct((1, 64), F32), jax...  74.8 us
    pallas_call x1, Pallas kernels, shards(): pl.pallas_call(hand_on, out_shape=(jax.ShapeDtypeStruct((1, 64), F32), ja...  1.85 us

profile of v3, /device:TPU:1, one launch (start us, length us, event | category | flops | bytes accessed | tf_op | source)
XLA Modules:
  0.0 78.6 jit_solution(15239015196190084099)
XLA Ops:
  1.9 74.8 %shard_map.76 = (f32[1,64]{1,0:T(1,128)}, f32[64,1024]{1,0:T(8,128)}, f32[64,1024]{1,0:T(8,128)}) custom-call(f32[64,1024]{1,0:T(8,128)} %video_any.1, f32[64,1024]{1,0:T(8,128)} %text_any.1, s32[64]{0:T(128)} %ids_any.1, f32[1]{0:T(128)S(6)} %copy.8.log_scale_any, f32[1]{0:T(128)S(6)} %copy.9.bias_any), custom_call_target="tpu_custom_call" | custom-call | flops 19327352832 | bytes 1048576 | tf_op jit(solution)/shard_map/pallas_call | solution.py:605
  76.8 1.8 %shard_map.77 = (f32[1,64]{1,0:T(1,128)}, f32[64,1024]{1,0:T(8,128)}, f32[64,1024]{1,0:T(8,128)}) custom-call(f32[1,64]{1,0:T(1,128)} %get-tuple-element.9.loss_ref, f32[64,1024]{1,0:T(8,128)} %get-tuple-element.10.vgrad_ref, f32[64,1024]{1,0:T(8,128)} %get-tuple-element.11.tgrad_ref), custom_call_target="tpu_custom_call" | custom-call | tf_op jit(solution)/shard_map/pallas_call | solution.py:657

commit v4 on v3

--- a/solution.py
+++ b/solution.py
@@ -56,17 +56,14 @@
 
 def video_row(hg, half, way, who):
     if isinstance(hg, int) and hg == 3:
-        return 768 + 128 * way + 64 * half + 32 * who
-    return 256 * hg + 128 * half + 64 * way + 32 * who
+        return 896 * way + 64 * half + 32 * who
+    return 128 + 256 * hg + 128 * half + 64 * way + 32 * who
 
 
 def text_row(slot):
     if slot[0] == OWN:
-        return 896 + 32 * slot[1] + 16 * slot[2]
-    way, tick = slot
-    if tick == 14:
-        return 960 + 16 * way
-    return 128 * (tick // 2) + 32 * way + 16 * (tick % 2)
+        return 32 * slot[1] + 16 * slot[2]
+    return 64 * (slot[1] + 1) + 16 * slot[0]
 
 
 def dot_nn(a, b):
@@ -146,11 +143,11 @@
 
     loads[0].wait()
     tu = unit(text_ref, inv_t)
-    tf[rows(896, 64), :] = tu
+    tf[rows(0, 64), :] = tu
     loads[1].wait()
     vu = unit(video_ref, inv_v)
     for half in range(2):
-        vf[rows(768 + 64 * half, 32), :] = vu[32 * half : 32 * half + 32]
+        vf[rows(64 * half, 32), :] = vu[32 * half : 32 * half + 32]
     lane = lax.broadcasted_iota(jnp.int32, (1, 128), 1)
     loads[2].wait()
     for quarter in range(4):
@@ -167,6 +164,10 @@
             device_id=t_out[way], device_id_type=MESH,
         )
 
+    def v_slot(tick, way):
+        q = tick % 4
+        return 128 + 256 * (tick // 4) + 128 * (q // 2) + 64 * way + 16 * (q % 2)
+
     def z_copy(way, tick, src, dst):
         return pltpu.make_async_remote_copy(
             src_ref=vf.at[rows(src, 16)], dst_ref=vf.at[rows(dst, 16)],
@@ -201,16 +202,16 @@
         ix_copy(d).start()
     ids_all[0, 0] = ids_own[...]
     for part in range(2):
+        for way in range(2):
+            for q in (2 * part, 2 * part + 1):
+                z_copy(way, q, 64 * (q // 2) + 16 * (q % 2), v_slot(q, way)).start()
         for way in range(4):
             t_copy((way, part)).start()
-        for way in range(2):
-            for q in (2 * part, 2 * part + 1):
-                z_copy(way, q, 768 + 64 * (q // 2) + 16 * (q % 2), 128 * (q // 2) + 64 * way + 16 * (q % 2)).start()
     for k in range(2, 4):
         for way in range(4):
             t_copy((way, k)).start()
     for q in range(4):
-        s_copy(q // 2, 14 + q % 2, 768 + 64 * (q // 2) + 16 * (q % 2)).start()
+        s_copy(q // 2, 14 + q % 2, 64 * (q // 2) + 16 * (q % 2)).start()
 
     local = lax.broadcasted_iota(jnp.int32, (32, 128), 0)
     for hg in range(4):
@@ -244,10 +245,6 @@
         vh[rows(start, size), :] = hi
         v8[0, rows(start, size), :] = (full * HI8).astype(F8)
         v8[1, rows(start, size), :] = (lo * LO8).astype(F8)
-
-    def v_slot(tick, way):
-        q = tick % 4
-        return 256 * (tick // 4) + 128 * (q // 2) + 64 * way + 16 * (q % 2)
 
     def place(n):
         if isinstance(n, int):
@@ -291,12 +288,12 @@
     def group_ids(group):
         vec = jnp.zeros((1, 128), jnp.int32)
         for spot in range(8):
-            if group < 7:
-                slot = (spot // 2, 2 * group + spot % 2)
-            elif spot < 4:
+            if spot >= 4:
+                slot = (spot - 4, 2 * group)
+            elif group > 0:
+                slot = (spot, 2 * group - 1)
+            else:
                 slot = (OWN, spot // 2, spot % 2)
-            else:
-                slot = (spot - 4, 14)
             dx, dy, half, part = identity(slot)
             ids = ids_all[dy, dx, pl.ds(2 * half + part, 1), :]
             vec = ids if spot == 0 else jnp.where(lane < 16 * spot, vec, ids)
@@ -304,12 +301,49 @@
 
     def count(tick):
         done = 0
-        for bound, more in ((4, 1), (8, 1), (9, 1), (10, 1), (12, 2), (13, 2), (14, 8)):
+        for bound, more in ((2, 1), (6, 1), (7, 1), (8, 1), (10, 2), (11, 1), (12, 1), (13, 1), (14, 7)):
             done = done + jnp.where(tick >= bound, more, 0)
         return done
 
     @pl.loop(0, 15)
     def _(tick):
+        for way in range(2):
+
+            @pl.when(tick < 12)
+            def _():
+                slot = v_slot(tick, way)
+                z_copy(way, tick, slot, slot).wait_recv()
+
+                @pl.when(tick < 8)
+                def _():
+                    z_copy(way, tick + 4, slot, slot + 256).start()
+
+                @pl.when((tick >= 8) & ((tick % 4) // 2 == way))
+                def _():
+                    last = 896 + 64 * way + 16 * (tick % 2)
+                    z_copy(way, 12 + tick % 2, slot, last).start()
+
+                s_copy(way, tick, slot).start()
+
+            @pl.when((tick == 12) | (tick == 13))
+            def _():
+                slot = 896 + 64 * way + 16 * (tick % 2)
+                z_copy(way, tick, slot, slot).wait_recv()
+                s_copy(way, tick, slot).start()
+
+            @pl.when((tick >= 1) & (tick <= 12))
+            def _():
+                s_copy(way, tick - 1, v_slot(tick - 1, way)).wait_recv()
+
+            @pl.when(tick >= 13)
+            def _():
+                s_copy(way, tick - 1, 896 + 64 * way + 16 * ((tick - 1) % 2)).wait_recv()
+
+            @pl.when(tick == 1)
+            def _():
+                for part in range(2):
+                    s_copy(way, 14 + part, 64 * way + 16 * part).wait_recv()
+
         for k in range(15):
 
             @pl.when(tick == k)
@@ -329,65 +363,15 @@
                     for group in range(8):
                         ids_vec[group] = group_ids(group)
 
-        for way in range(2):
-
-            @pl.when(tick < 12)
-            def _():
-                slot = v_slot(tick, way)
-                z_copy(way, tick, slot, slot).wait_recv()
-
-                @pl.when(tick < 8)
-                def _():
-                    z_copy(way, tick + 4, slot, slot + 256).start()
-
-                @pl.when((tick >= 8) & ((tick % 4) // 2 == way))
-                def _():
-                    last = 896 + 64 * way + 16 * (tick % 2)
-                    z_copy(way, 12 + tick % 2, slot, last).start()
-
-                s_copy(way, tick, slot).start()
-
-            @pl.when((tick == 12) | (tick == 13))
-            def _():
-                slot = 896 + 64 * way + 16 * (tick % 2)
-                z_copy(way, tick, slot, slot).wait_recv()
-                s_copy(way, tick, slot).start()
-
-            @pl.when((tick >= 1) & (tick <= 12))
-            def _():
-                s_copy(way, tick - 1, v_slot(tick - 1, way)).wait_recv()
-
-            @pl.when(tick >= 13)
-            def _():
-                s_copy(way, tick - 1, 896 + 64 * way + 16 * ((tick - 1) % 2)).wait_recv()
-
-            @pl.when(tick == 1)
-            def _():
-                for part in range(2):
-                    s_copy(way, 14 + part, 768 + 64 * way + 16 * part).wait_recv()
-
-        @pl.when(tick == 0)
-        def _():
-            t_split(896, 64)
-
-        @pl.when(tick % 2 == 1)
-        def _():
-            t_split(128 * (tick // 2), 128)
-
-        @pl.when((tick % 2 == 0) & (tick >= 2) & (tick <= 12))
-        def _():
-            v_split(128 * (tick // 2 - 1), 128)
-
-        @pl.when(tick == 1)
-        def _():
-            v_split(768, 128)
-
-        @pl.when(tick == 14)
-        def _():
-            v_split(896, 128)
-            t_split(960, 64)
-
-        @pl.when(tick == 4)
+        @pl.when(tick % 2 == 0)
+        def _():
+            t_split(64 * tick, 128)
+
+        @pl.when((tick == 1) | ((tick % 2 == 0) & (tick >= 2)))
+        def _():
+            v_split(jnp.where(tick == 1, 0, 64 * tick), 128)
+
+        @pl.when(tick == 2)
         def _():
             block_dots(0)
 
@@ -437,7 +421,7 @@
 
     def z_pump(hg, half, with_recv):
         for way in range(2):
-            slot = 256 * hg + 128 * half + 64 * way
+            slot = video_row(hg, half, way, 0)
             rs_copy(hg, half, way).wait_recv()
             if with_recv[way]:
                 rz_copy(way, half, hg + 1, slot).wait_recv()
@@ -468,7 +452,7 @@
     def l_copy(hg, way, who, owner):
         slot = (hg * 2 + way) * 2 + who
         return pltpu.make_async_remote_copy(
-            src_ref=lrow.at[hg], dst_ref=lrecv.at[slot],
+            src_ref=lrow.at[pl.ds(1 + 2 * hg if hg < 3 else 6 * way, 2)], dst_ref=lrecv.at[slot],
             send_sem=l_send.at[0], recv_sem=l_recv.at[slot],
             device_id=owner, device_id_type=MESH,
         )
@@ -488,11 +472,12 @@
 
     t_grad(7)
     t_pump(14)
+    t_pump(13)
 
     @pl.loop(0, 7)
     def _(i):
         hg, half = 2 - (i - 1) // 2, (i - 1) % 2
-        v_grad(jnp.where(i == 0, 7, 2 * hg + half))
+        v_grad(jnp.where(i == 0, 7, 1 + 2 * hg + half))
 
         @pl.when(i == 0)
         def _():
@@ -505,52 +490,53 @@
                 rs_copy(hg, half, way).start()
 
         t_grad(6 - i)
+        @pl.when(i == 0)
+        def _():
+            z_last()
+
+        @pl.when(i == 1)
+        def _():
+            z_pump(2, 0, (True, False))
+
+        @pl.when(i == 2)
+        def _():
+            z_pump(2, 1, (False, True))
+
+        @pl.when(i >= 3)
+        def _():
+            z_pump(hg, half, (True, True))
+
         for k in range(7):
 
             @pl.when(i == k)
             def _():
-                t_pump(13 - 2 * k)
                 t_pump(12 - 2 * k)
-
-        @pl.when(i == 0)
-        def _():
-            z_last()
-
-        @pl.when(i == 1)
-        def _():
-            z_pump(2, 0, (True, False))
-
-        @pl.when(i == 2)
-        def _():
-            z_pump(2, 1, (False, True))
-
-        @pl.when(i >= 3)
-        def _():
-            z_pump(hg, half, (True, True))
+                if k < 6:
+                    t_pump(11 - 2 * k)
 
         @pl.when(i == 3)
         def _():
             for m in range(8):
                 turned = jnp.transpose(lacc[rows(m * 128, 128), :])
-                lrow[m // 2, m % 2 : m % 2 + 1, :] = jnp.sum(turned, axis=0, keepdims=True)
+                lrow[m] = jnp.sum(turned, axis=0, keepdims=True)
             for hg_, way, who, owner in l_peers():
                 l_copy(hg_, way, who, owner).start()
 
-    v_grad(6)
+    v_grad(0)
     for half in range(2):
         rs_copy(3, half, 0).start()
 
-    loss = [lrow[3, 0:1, 64 * half : 64 * half + 32] for half in range(2)]
+    loss = [lrow[0, :, 64 * half : 64 * half + 32] for half in range(2)]
     for hg, way, who, owner in l_peers():
         l_copy(hg, way, who, owner).wait_recv()
         part = lrecv.at[(hg * 2 + way) * 2 + who]
         for half in range(2):
             if hg < 3:
                 first = 64 * way + 32 * who
-                loss[half] = loss[half] + part[half : half + 1, first : first + 32]
+                loss[half] = loss[half] + part[half, :, first : first + 32]
             else:
                 first = 64 * half + 32 * who
-                loss[half] = loss[half] + part[way : way + 1, first : first + 32]
+                loss[half] = loss[half] + part[way, :, first : first + 32]
     loss_ref[:, :32] = loss[0]
     loss_ref[:, 32:] = loss[1]
 
@@ -564,7 +550,7 @@
             tgrad_ref[rows(first, 16), :] = back * inv_t[rows(first, 16), :1]
 
     for half in range(2):
-        own = 768 + 64 * half
+        own = 64 * half
         rs_copy(3, half, 0).wait_recv()
         total = vg[rows(own, 32), :] + recv_s[3, half, 0]
         for way in range(2):
@@ -631,8 +617,8 @@
             pltpu.VMEM((8, 1, 128), jnp.int32),
             pltpu.VMEM((1024, 128), jnp.int32),
             pltpu.VMEM((1024, 128), F32),
-            pltpu.VMEM((4, 2, 128), F32),
-            pltpu.VMEM((16, 2, 128), F32),
+            pltpu.VMEM((8, 1, 128), F32),
+            pltpu.VMEM((16, 2, 1, 128), F32),
             pltpu.VMEM((64, 128), F32),
             pltpu.VMEM((64, 128), F32),
             pltpu.VMEM((64, 1024), F32),

time: 78.7 us -> 78.1 us (level)
  no operation moved by 1% of the time
where the time goes in v4:
time: 78.1 us; the launch traced here: 78 us
  Pallas kernels  76 us (97%)
  between operations  1.93 us (2%)
    pallas_call x1, Pallas kernels, shards(): pl.pallas_call(kernel, out_shape=(jax.ShapeDtypeStruct((1, 64), F32), jax...  74.2 us
    pallas_call x1, Pallas kernels, shards(): pl.pallas_call(hand_on, out_shape=(jax.ShapeDtypeStruct((1, 64), F32), ja...  1.85 us

profile of v4, /device:TPU:1, one launch (start us, length us, event | category | flops | bytes accessed | tf_op | source)
XLA Modules:
  0.0 78.0 jit_solution(463664159924666180)
XLA Ops:
  1.9 74.2 %shard_map.76 = (f32[1,64]{1,0:T(1,128)}, f32[64,1024]{1,0:T(8,128)}, f32[64,1024]{1,0:T(8,128)}) custom-call(f32[64,1024]{1,0:T(8,128)} %video_any.1, f32[64,1024]{1,0:T(8,128)} %text_any.1, s32[64]{0:T(128)} %ids_any.1, f32[1]{0:T(128)S(6)} %copy.8.log_scale_any, f32[1]{0:T(128)S(6)} %copy.9.bias_any), custom_call_target="tpu_custom_call" | custom-call | flops 19327352832 | bytes 1048576 | tf_op jit(solution)/shard_map/pallas_call | solution.py:591
  76.1 1.8 %shard_map.77 = (f32[1,64]{1,0:T(1,128)}, f32[64,1024]{1,0:T(8,128)}, f32[64,1024]{1,0:T(8,128)}) custom-call(f32[1,64]{1,0:T(1,128)} %get-tuple-element.9.loss_ref, f32[64,1024]{1,0:T(8,128)} %get-tuple-element.10.vgrad_ref, f32[64,1024]{1,0:T(8,128)} %get-tuple-element.11.tgrad_ref), custom_call_target="tpu_custom_call" | custom-call | tf_op jit(solution)/shard_map/pallas_call | solution.py:643

commit v5 on v4

--- a/solution.py
+++ b/solution.py
@@ -131,9 +131,8 @@
     for peer in line_x[1:] + line_y[1:]:
         pl.semaphore_signal(barrier, inc=1, device_id=peer, device_id_type=MESH)
     pl.semaphore_signal(barrier, inc=1, device_id=other, device_id_type=MESH)
-    for step in range(1, 8):
-        for c in range(2):
-            pl.semaphore_signal(barrier, inc=1, device_id=at(x, y, (z + step) % 8, c), device_id_type=MESH)
+    for peer in z_out:
+        pl.semaphore_signal(barrier, inc=1, device_id=peer, device_id_type=MESH)
 
     def unit(ref, inv_ref):
         full = ref[...]
@@ -196,7 +195,7 @@
             device_id=line_y[d], device_id_type=MESH,
         )
 
-    pl.semaphore_wait(barrier, 21)
+    pl.semaphore_wait(barrier, 9)
 
     for d in range(1, 4):
         ix_copy(d).start()
@@ -266,16 +265,13 @@
     def block_rest(n):
         vb, tb = place(n)
         vs = rows(vb * 256, 256)
-        total = jnp.zeros((256, 128), F32)
+        es = []
         for half in range(2):
             logits = dots[:, 128 * half : 128 * half + 128] * scale + bias
             match = vidx[vs, :] == ids_vec[tb * 2 + half]
-            q = jnp.where(match, -logits, logits)
-            e = jnp.exp(q)
-            u = 1.0 + e
-            weight = (jnp.where(match, -scale, scale) * e) / u
-            small = e * (1.0 - e * (0.5 - e * (1.0 / 3.0)))
-            total = total + jnp.where(e < 1.0 / 64.0, small, jnp.log(u))
+            e = jnp.exp(jnp.where(match, -logits, logits))
+            es.append(e)
+            weight = (jnp.where(match, -scale, scale) * e) / (1.0 + e)
             hi, lo = split(weight)
             hi8, lo8 = (weight * W_HI8).astype(F8), (lo * W_LO8).astype(F8)
             cols = rows((tb * 2 + half) * 128, 128)
@@ -283,7 +279,9 @@
                 w[vb * 2 + k, :, cols] = hi[128 * k : 128 * k + 128]
                 w8[0, vb * 2 + k, :, cols] = hi8[128 * k : 128 * k + 128]
                 w8[1, vb * 2 + k, :, cols] = lo8[128 * k : 128 * k + 128]
-        lacc[vs, :] += total
+        both = es[0] + es[1] + es[0] * es[1]
+        small = both * (1.0 - both * (0.5 - both * (1.0 / 3.0)))
+        lacc[vs, :] += jnp.where(both < 1.0 / 64.0, small, jnp.log(1.0 + both))
 
     def group_ids(group):
         vec = jnp.zeros((1, 128), jnp.int32)
@@ -301,7 +299,7 @@
 
     def count(tick):
         done = 0
-        for bound, more in ((2, 1), (6, 1), (7, 1), (8, 1), (10, 2), (11, 1), (12, 1), (13, 1), (14, 7)):
+        for bound, more in ((2, 1), (6, 1), (7, 1), (8, 1), (10, 2), (11, 1), (12, 1), (13, 1), (14, 4)):
             done = done + jnp.where(tick >= bound, more, 0)
         return done
 
@@ -380,7 +378,7 @@
             block_rest(n - 1)
             block_dots(n)
 
-    block_rest(15)
+    block_rest(12)
 
     def rt_copy(slot):
         way, tick = slot
@@ -473,6 +471,11 @@
     t_grad(7)
     t_pump(14)
     t_pump(13)
+
+    @pl.loop(13, 16)
+    def _(n):
+        block_dots(n)
+        block_rest(n)
 
     @pl.loop(0, 7)
     def _(i):
@@ -578,10 +581,21 @@
     drain(lrecv.at[pl.ds(0, 15)], l_send.at[0])
 
 
-def hand_on(loss_ref, vgrad_ref, tgrad_ref, loss_out, vgrad_out, tgrad_out):
-    loss_out[...] = loss_ref[...]
-    vgrad_out[...] = vgrad_ref[...]
-    tgrad_out[...] = tgrad_ref[...]
+def hand_on(loss_any, vgrad_any, tgrad_any, loss_out, vgrad_out, tgrad_out, loss, grads, sems):
+    pieces = [(loss_any, loss, loss_out)]
+    for n, (src, dst) in enumerate(((vgrad_any, vgrad_out), (tgrad_any, tgrad_out))):
+        for part in range(2):
+            here = pl.ds(32 * part, 32)
+            pieces.append((src.at[here], grads.at[n, here], dst.at[here]))
+    first = [pltpu.make_async_copy(a, b, sems.at[0, n]) for n, (a, b, _) in enumerate(pieces)]
+    second = [pltpu.make_async_copy(b, c, sems.at[1, n]) for n, (_, b, c) in enumerate(pieces)]
+    for copy in first:
+        copy.start()
+    for come, go in zip(first, second):
+        come.wait()
+        go.start()
+    for copy in second:
+        copy.wait()
 
 
 def shards(video, text, match_ids, log_scale, bias):
@@ -647,8 +661,9 @@
             jax.ShapeDtypeStruct((64, 1024), F32),
             jax.ShapeDtypeStruct((64, 1024), F32),
         ),
-        in_specs=[vmem] * 3,
-        out_specs=(vmem,) * 3,
+        in_specs=[hbm] * 3,
+        out_specs=(hbm,) * 3,
+        scratch_shapes=[pltpu.VMEM((1, 64), F32), pltpu.VMEM((2, 64, 1024), F32), dma((2, 5))],
     )(loss, vgrad, tgrad)
     return loss.reshape(64), vgrad, tgrad
 

time: 78.1 us -> 76.4 us (0.978)
  Pallas kernels: 76 us -> 74.3 us
    pallas_call x1, Pallas kernels: 74.2 us -> 72.5 us  [shards(): pl.pallas_call(kernel, out_shape=(jax.ShapeDtypeStruct((1, 64), F32), jax...]
where the time goes in v5:
time: 76.4 us; the launch traced here: 76.2 us
  Pallas kernels  74.3 us (97%)
  between operations  1.93 us (3%)
    pallas_call x1, Pallas kernels, shards(): pl.pallas_call(kernel, out_shape=(jax.ShapeDtypeStruct((1, 64), F32), jax...  72.5 us
    pallas_call x1, Pallas kernels, shards(): pl.pallas_call(hand_on, out_shape=(jax.ShapeDtypeStruct((1, 64), F32), ja...  1.84 us

profile of v5, /device:TPU:1, one launch (start us, length us, event | category | flops | bytes accessed | tf_op | source)
XLA Modules:
  0.0 76.2 jit_solution(12712831211980161165)
XLA Ops:
  1.9 72.5 %shard_map.76 = (f32[1,64]{1,0:T(1,128)}, f32[64,1024]{1,0:T(8,128)}, f32[64,1024]{1,0:T(8,128)}) custom-call(f32[64,1024]{1,0:T(8,128)} %video_any.1, f32[64,1024]{1,0:T(8,128)} %text_any.1, s32[64]{0:T(128)} %ids_any.1, f32[1]{0:T(128)S(6)} %copy.8.log_scale_any, f32[1]{0:T(128)S(6)} %copy.9.bias_any), custom_call_target="tpu_custom_call" | custom-call | flops 19327352832 | bytes 1048576 | tf_op jit(solution)/shard_map/pallas_call | solution.py:605
  74.4 1.8 %shard_map.77 = (f32[1,64]{1,0:T(1,128)}, f32[64,1024]{1,0:T(8,128)}, f32[64,1024]{1,0:T(8,128)}) custom-call(f32[1,64]{1,0:T(1,128)} %get-tuple-element.9.loss_any, f32[64,1024]{1,0:T(8,128)} %get-tuple-element.10.vgrad_any, f32[64,1024]{1,0:T(8,128)} %get-tuple-element.11.tgrad_any), custom_call_target="tpu_custom_call" | custom-call | tf_op jit(solution)/shard_map/pallas_call | solution.py:657

commit v6 on v5

--- a/solution.py
+++ b/solution.py
@@ -254,20 +254,18 @@
         r = n - m * m
         return jnp.where(r <= m, r, m), jnp.where(r <= m, m, r - m - 1)
 
-    def block_dots(n):
-        vb, tb = place(n)
-        vs, ts = rows(vb * 256, 256), rows(tb * 256, 256)
+    def some_dots(start, size, tb):
+        vs, ts = rows(start, size), rows(tb * 256, 256)
         small = dot_nt(
             jnp.concatenate([v8[0, vs, :], v8[1, vs, :]], axis=1), jnp.concatenate([t8[0, ts, :], t8[1, ts, :]], axis=1)
         )
-        dots[...] = dot_nt(vh[vs, :], th[ts, :]) + small * (1.0 / (HI8 * LO8))
-
-    def block_rest(n):
-        vb, tb = place(n)
-        vs = rows(vb * 256, 256)
+        dots[:size, :] = dot_nt(vh[vs, :], th[ts, :]) + small * (1.0 / (HI8 * LO8))
+
+    def some_rest(start, size, tb):
+        vs = rows(start, size)
         es = []
         for half in range(2):
-            logits = dots[:, 128 * half : 128 * half + 128] * scale + bias
+            logits = dots[:size, 128 * half : 128 * half + 128] * scale + bias
             match = vidx[vs, :] == ids_vec[tb * 2 + half]
             e = jnp.exp(jnp.where(match, -logits, logits))
             es.append(e)
@@ -275,13 +273,21 @@
             hi, lo = split(weight)
             hi8, lo8 = (weight * W_HI8).astype(F8), (lo * W_LO8).astype(F8)
             cols = rows((tb * 2 + half) * 128, 128)
-            for k in range(2):
-                w[vb * 2 + k, :, cols] = hi[128 * k : 128 * k + 128]
-                w8[0, vb * 2 + k, :, cols] = hi8[128 * k : 128 * k + 128]
-                w8[1, vb * 2 + k, :, cols] = lo8[128 * k : 128 * k + 128]
+            for k in range(size // 128):
+                w[start // 128 + k, :, cols] = hi[128 * k : 128 * k + 128]
+                w8[0, start // 128 + k, :, cols] = hi8[128 * k : 128 * k + 128]
+                w8[1, start // 128 + k, :, cols] = lo8[128 * k : 128 * k + 128]
         both = es[0] + es[1] + es[0] * es[1]
         small = both * (1.0 - both * (0.5 - both * (1.0 / 3.0)))
         lacc[vs, :] += jnp.where(both < 1.0 / 64.0, small, jnp.log(1.0 + both))
+
+    def block_dots(n):
+        vb, tb = place(n)
+        some_dots(vb * 256, 256, tb)
+
+    def block_rest(n):
+        vb, tb = place(n)
+        some_rest(vb * 256, 256, tb)
 
     def group_ids(group):
         vec = jnp.zeros((1, 128), jnp.int32)
@@ -299,7 +305,7 @@
 
     def count(tick):
         done = 0
-        for bound, more in ((2, 1), (6, 1), (7, 1), (8, 1), (10, 2), (11, 1), (12, 1), (13, 1), (14, 4)):
+        for bound, more in ((2, 1), (6, 1), (7, 1), (8, 1), (10, 2), (11, 1), (12, 1), (13, 1)):
             done = done + jnp.where(tick >= bound, more, 0)
         return done
 
@@ -378,7 +384,12 @@
             block_rest(n - 1)
             block_dots(n)
 
-    block_rest(12)
+    block_rest(8)
+
+    @pl.loop(0, 1)
+    def _(n):
+        some_dots(n * 1024, 1024, 3)
+        some_rest(n * 1024, 1024, 3)
 
     def rt_copy(slot):
         way, tick = slot
@@ -519,9 +530,11 @@
 
         @pl.when(i == 3)
         def _():
+            ones = jnp.ones((16, 128), BF16)
+            hi, lo = split(lacc[...])
+            sums = dot_nt(ones, hi) + dot_nt(ones, lo.astype(BF16))
             for m in range(8):
-                turned = jnp.transpose(lacc[rows(m * 128, 128), :])
-                lrow[m] = jnp.sum(turned, axis=0, keepdims=True)
+                lrow[m] = sums[:1, 128 * m : 128 * m + 128]
             for hg_, way, who, owner in l_peers():
                 l_copy(hg_, way, who, owner).start()
 
@@ -618,7 +631,7 @@
             pltpu.VMEM((2, 1024, 1024), F8),
             pltpu.VMEM((1024, 1024), BF16),
             pltpu.VMEM((2, 1024, 1024), F8),
-            pltpu.VMEM((256, 256), F32),
+            pltpu.VMEM((1024, 256), F32),
             pltpu.VMEM((8, 128, 1024), BF16),
             pltpu.VMEM((2, 8, 128, 1024), F8),
             pltpu.VMEM((1024, 1024), F32),

time: 76.4 us -> 76.1 us (level)
  no operation moved by 1% of the time
where the time goes in v6:
time: 76.1 us; the launch traced here: 75.9 us
  Pallas kernels  74 us (97%)
  between operations  1.93 us (3%)
    pallas_call x1, Pallas kernels, shards(): pl.pallas_call(kernel, out_shape=(jax.ShapeDtypeStruct((1, 64), F32), jax...  72.2 us
    pallas_call x1, Pallas kernels, shards(): pl.pallas_call(hand_on, out_shape=(jax.ShapeDtypeStruct((1, 64), F32), ja...  1.84 us

profile of v6, /device:TPU:1, one launch (start us, length us, event | category | flops | bytes accessed | tf_op | source)
XLA Modules:
  0.0 75.9 jit_solution(6063459776258267615)
XLA Ops:
  1.9 72.2 %shard_map.76 = (f32[1,64]{1,0:T(1,128)}, f32[64,1024]{1,0:T(8,128)}, f32[64,1024]{1,0:T(8,128)}) custom-call(f32[64,1024]{1,0:T(8,128)} %video_any.1, f32[64,1024]{1,0:T(8,128)} %text_any.1, s32[64]{0:T(128)} %ids_any.1, f32[1]{0:T(128)S(6)} %copy.8.log_scale_any, f32[1]{0:T(128)S(6)} %copy.9.bias_any), custom_call_target="tpu_custom_call" | custom-call | flops 19327352832 | bytes 1048576 | tf_op jit(solution)/shard_map/pallas_call | solution.py:618
  74.1 1.8 %shard_map.77 = (f32[1,64]{1,0:T(1,128)}, f32[64,1024]{1,0:T(8,128)}, f32[64,1024]{1,0:T(8,128)}) custom-call(f32[1,64]{1,0:T(1,128)} %get-tuple-element.9.loss_any, f32[64,1024]{1,0:T(8,128)} %get-tuple-element.10.vgrad_any, f32[64,1024]{1,0:T(8,128)} %get-tuple-element.11.tgrad_any), custom_call_target="tpu_custom_call" | custom-call | tf_op jit(solution)/shard_map/pallas_call | solution.py:670

commit v7 on v6

--- a/solution.py
+++ b/solution.py
@@ -339,7 +339,7 @@
             def _():
                 s_copy(way, tick - 1, v_slot(tick - 1, way)).wait_recv()
 
-            @pl.when(tick >= 13)
+            @pl.when(tick == 13)
             def _():
                 s_copy(way, tick - 1, 896 + 64 * way + 16 * ((tick - 1) % 2)).wait_recv()
 
@@ -371,7 +371,7 @@
         def _():
             t_split(64 * tick, 128)
 
-        @pl.when((tick == 1) | ((tick % 2 == 0) & (tick >= 2)))
+        @pl.when((tick == 1) | ((tick % 2 == 0) & (tick >= 2) & (tick <= 12)))
         def _():
             v_split(jnp.where(tick == 1, 0, 64 * tick), 128)
 
@@ -384,7 +384,14 @@
             block_rest(n - 1)
             block_dots(n)
 
-    block_rest(8)
+        @pl.when(tick == 13)
+        def _():
+            block_rest(8)
+            for way in range(2):
+                s_copy(way, 13, 896 + 64 * way + 16).wait_recv()
+            v_split(896, 128)
+            block_dots(13)
+            block_rest(13)
 
     @pl.loop(0, 1)
     def _(n):
@@ -483,7 +490,7 @@
     t_pump(14)
     t_pump(13)
 
-    @pl.loop(13, 16)
+    @pl.loop(14, 16)
     def _(n):
         block_dots(n)
         block_rest(n)

time: 76.1 us -> 75.5 us (level)
  no operation moved by 1% of the time
where the time goes in v7:
time: 75.5 us; the launch traced here: 75.4 us
  Pallas kernels  73.5 us (97%)
  between operations  1.93 us (3%)
    pallas_call x1, Pallas kernels, shards(): pl.pallas_call(kernel, out_shape=(jax.ShapeDtypeStruct((1, 64), F32), jax...  71.6 us
    pallas_call x1, Pallas kernels, shards(): pl.pallas_call(hand_on, out_shape=(jax.ShapeDtypeStruct((1, 64), F32), ja...  1.84 us

profile of v7, /device:TPU:1, one launch (start us, length us, event | category | flops | bytes accessed | tf_op | source)
XLA Modules:
  0.0 75.4 jit_solution(6228035001444138161)
XLA Ops:
  1.9 71.6 %shard_map.76 = (f32[1,64]{1,0:T(1,128)}, f32[64,1024]{1,0:T(8,128)}, f32[64,1024]{1,0:T(8,128)}) custom-call(f32[64,1024]{1,0:T(8,128)} %video_any.1, f32[64,1024]{1,0:T(8,128)} %text_any.1, s32[64]{0:T(128)} %ids_any.1, f32[1]{0:T(128)S(6)} %copy.8.log_scale_any, f32[1]{0:T(128)S(6)} %copy.9.bias_any), custom_call_target="tpu_custom_call" | custom-call | flops 19327352832 | bytes 1048576 | tf_op jit(solution)/shard_map/pallas_call | solution.py:625
  73.6 1.8 %shard_map.77 = (f32[1,64]{1,0:T(1,128)}, f32[64,1024]{1,0:T(8,128)}, f32[64,1024]{1,0:T(8,128)}) custom-call(f32[1,64]{1,0:T(1,128)} %get-tuple-element.9.loss_any, f32[64,1024]{1,0:T(8,128)} %get-tuple-element.10.vgrad_any, f32[64,1024]{1,0:T(8,128)} %get-tuple-element.11.tgrad_any), custom_call_target="tpu_custom_call" | custom-call | tf_op jit(solution)/shard_map/pallas_call | solution.py:677
